TPU v7x, 32 devices: a whole 2x2x4 slice. The times are simulated.
32 devices in a mesh: freq: 4 (over y, core), sky: 8 (over z, x).
Axes of the slice: x: 2, y: 2, z: 4, core: 2. Of those that a mesh axis runs over, the one named last changes fastest.
Arguments:
- sky_cube: bfloat16 [256, 256, 1024], P(None, 'sky', 'freq'), may hold values from -6 to 6
- weight_first: bfloat16 [3, 3, 1024, 256], P(None, None, 'freq'), may hold values from -0.0625 to 0.0625
- weight_second: bfloat16 [3, 3, 256, 256], replicated, may hold values from -0.125 to 0.125
- cotangent: bfloat16 [256, 256, 256], P('freq', 'sky'), may hold values from -0.0234375 to 0.0234375
Outputs:
- features: bfloat16 [256, 256, 256], P('freq', 'sky')
- grad_first: float32 [3, 3, 1024, 256], P(None, None, 'freq')
- grad_second: float32 [3, 3, 256, 256], replicated
All inputs are finite; a program needn't handle non-finite values.
Results may differ from a plain program's by a relative error of at most 0.024.
Values may be sent and summed in bfloat16 or wider, within the bound.
A program may use at most 128 MiB of HBM per device.

v0:
```python
import jax
import jax.numpy as jnp
from jax import lax
from jax.sharding import PartitionSpec as P


def with_halo(x, sides, width):
    for axis, dim in sides:
        count, length = (lax.axis_size(axis), x.shape[dim])
        up = [(i, (i + 1) % count) for i in range(count - 1)]
        down = [(j, i) for i, j in up]
        last = lax.slice_in_dim(x, length - width, length, axis=dim)
        first = lax.slice_in_dim(x, 0, width, axis=dim)
        before = lax.ppermute(last, axis, up)
        after = lax.ppermute(first, axis, down)
        x = jnp.concatenate([before, x, after], axis=dim)
    return x


def conv_taps(padded, kernel, col_count, row_count):
    total = jnp.zeros((col_count * row_count, kernel.shape[3]), jnp.float32)
    for tap_col in range(3):
        for tap_row in range(3):
            piece = padded[tap_col : tap_col + col_count, tap_row : tap_row + row_count].reshape(
                col_count * row_count, -1
            )
            total = total + jnp.dot(
                piece, kernel[tap_col, tap_row], preferred_element_type=jnp.float32
            )
    return total.reshape(col_count, row_count, kernel.shape[3])


def conv_back(padded, kernel, col_count, row_count):
    total = jnp.zeros((col_count * row_count, kernel.shape[2]), jnp.float32)
    for tap_col in range(3):
        for tap_row in range(3):
            piece = padded[
                2 - tap_col : 2 - tap_col + col_count, 2 - tap_row : 2 - tap_row + row_count
            ].reshape(col_count * row_count, -1)
            total = total + lax.dot_general(
                piece,
                kernel[tap_col, tap_row],
                (((1,), (1,)), ((), ())),
                preferred_element_type=jnp.float32,
            )
    return total.reshape(col_count, row_count, kernel.shape[2])


def kernel_grad(padded, grads, col_count, row_count):
    flat = grads.reshape(col_count * row_count, -1)
    rows_out = []
    for tap_col in range(3):
        line = []
        for tap_row in range(3):
            piece = padded[tap_col : tap_col + col_count, tap_row : tap_row + row_count].reshape(
                col_count * row_count, -1
            )
            line.append(
                lax.dot_general(
                    piece, flat, (((0,), (0,)), ((), ())), preferred_element_type=jnp.float32
                )
            )
        rows_out.append(jnp.stack(line))
    return jnp.stack(rows_out)


def pad_columns(field):
    return jnp.pad(field, ((1, 1), (0, 0), (0, 0)))


def silu_slope(pre):
    sigma = jax.nn.sigmoid(pre)
    return sigma * (1.0 + pre * (1.0 - sigma))


def body(sky_cube, weight_first, weight_second, cotangent):
    row_count = sky_cube.shape[1]
    strip = cotangent.shape[0]
    cube_rows = with_halo(sky_cube, (("sky", 1),), 1)
    cube_pad = pad_columns(cube_rows)
    slab = cube_pad
    pre = lax.psum_scatter(
        conv_taps(slab, weight_first, strip * lax.axis_size("freq"), row_count).astype(
            jnp.bfloat16
        ),
        "freq",
        scatter_dimension=0,
        tiled=True,
    ).astype(jnp.float32)
    hidden = jax.nn.silu(pre).astype(jnp.bfloat16)
    hidden_pad = with_halo(hidden, (("freq", 0), ("sky", 1)), 1)
    features = conv_taps(hidden_pad, weight_second, strip, row_count).astype(jnp.bfloat16)
    cotan_pad = with_halo(cotangent, (("freq", 0), ("sky", 1)), 1)
    back = conv_back(cotan_pad, weight_second, strip, row_count)
    delta = (back * silu_slope(pre)).astype(jnp.bfloat16)
    second_part = kernel_grad(hidden_pad, cotangent, strip, row_count)
    piece = lax.all_gather(delta, "freq", axis=0, tiled=True)
    count = piece.shape[0]
    slab = cube_pad
    first_part = kernel_grad(slab, piece, count, row_count)
    grad_first = lax.psum(first_part.astype(jnp.bfloat16), "sky").astype(jnp.float32)
    grad_second = lax.psum(second_part, ("freq", "sky"))
    return (features, grad_first, grad_second)


def solution(mesh):
    return jax.shard_map(
        body,
        mesh=mesh,
        in_specs=(P(None, "sky", "freq"), P(None, None, "freq", None), P(), P("freq", "sky", None)),
        out_specs=(P("freq", "sky", None), P(None, None, "freq", None), P()),
        check_vma=False,
    )
```

profile of v0, /device:TPU:1, one launch (start us, length us, event | category | flops | bytes accessed | tf_op | source)
XLA Modules:
  0.0 492.8 jit_solution(15397694136639785615)
XLA Ops:
  7.2 7.6 %copy.25 = bf16[256,32,256]{0,2,1:T(8,128)(2,1)} copy(bf16[256,32,256]{2,1,0:T(8,128)(2,1)} %param.4) | data formatting | bytes 8388608 | tf_op args[0]
  17.1 4.6 collective-permute-start
  22.9 3.7 collective-permute-done
  26.6 7.9 %fusion.6 = bf16[258,34,256]{0,2,1:T(8,128)(2,1)} fusion(bf16[256,1,256]{0,2,1:T(8,128)(2,1)S(1)} %collective-permute-done.1, bf16[256,32,256]{0,2,1:T(8,128)(2,1)} %copy.25, bf16[256,1,256]{0,2,1:T(8,128)(2,1)S(1)} %collective-permute-done), kind=kLoop, calls=%fused_computation.16 | loop fusion | flops 26947584 | bytes 8947712 | tf_op jit(solution)/shard_map/concatenate | solution.py:16
  34.6 19.7 %fusion.144 = (bf16[256,32,256]{0,2,1:T(8,128)(2,1)}, bf16[256,32,256]{0,2,1:T(8,128)(2,1)}, bf16[256,32,256]{0,2,1:T(8,128)(2,1)}, bf16[256,32,256]{0,2,1:T(8,1...) fusion(bf16[258,34,256]{0,2,1:T(8,128)(2,1)} %fusion.6), kind=kLoop, calls=%fused_computation.207 | loop fusion | bytes 50331648 | tf_op jit(solution)/shard_map/slice | solution.py:24
  54.3 8.0 %copy.28 = bf16[256,32,256]{2,1,0:T(8,128)(2,1)} copy(bf16[256,32,256]{0,2,1:T(8,128)(2,1)} %get-tuple-element.8) | data formatting | bytes 8388608 | tf_op jit(solution)/shard_map/slice | solution.py:24
  62.3 7.9 %copy.29 = bf16[256,32,256]{2,1,0:T(8,128)(2,1)} copy(bf16[256,32,256]{0,2,1:T(8,128)(2,1)} %get-tuple-element.7) | data formatting | bytes 8388608 | tf_op jit(solution)/shard_map/slice | solution.py:24
  70.2 7.9 %copy.30 = bf16[256,32,256]{2,1,0:T(8,128)(2,1)} copy(bf16[256,32,256]{0,2,1:T(8,128)(2,1)} %get-tuple-element.6) | data formatting | bytes 8388608 | tf_op jit(solution)/shard_map/slice | solution.py:24
  78.1 5.9 %pad_maximum_fusion = (bf16[256,32,256]{0,2,1:T(8,128)(2,1)}, bf16[256,32,256]{0,2,1:T(8,128)(2,1)}) fusion(bf16[256,1,256]{0,2,1:T(8,128)(2,1)S(1)} %collective-permute-done.1, bf16[256,32,256]{0,2,1:T(8,128)(2,1)} %copy.25, bf16[256,1,256]{0,2,1:T(8,128)(2,1)S(1)} %collective-permute-done), kind=kLoop, calls=%fused_computation.25 | loop fusion | flops 4194304 | bytes 12845056 | tf_op jit(solution)/shard_map/slice | solution.py:24
  84.0 7.9 %copy.32 = bf16[256,32,256]{2,1,0:T(8,128)(2,1)} copy(bf16[256,32,256]{0,2,1:T(8,128)(2,1)} %get-tuple-element.10) | data formatting | bytes 8388608 | tf_op jit(solution)/shard_map/slice | solution.py:24
  91.9 7.9 %copy.34 = bf16[256,32,256]{2,1,0:T(8,128)(2,1)} copy(bf16[256,32,256]{0,2,1:T(8,128)(2,1)} %get-tuple-element.9) | data formatting | bytes 8388608 | tf_op jit(solution)/shard_map/slice | solution.py:24
  99.8 7.9 %copy.35 = bf16[256,32,256]{2,1,0:T(8,128)(2,1)} copy(bf16[256,32,256]{0,2,1:T(8,128)(2,1)} %get-tuple-element.5) | data formatting | bytes 8388608 | tf_op jit(solution)/shard_map/slice | solution.py:24
  107.8 8.0 %copy.36 = bf16[256,32,256]{2,1,0:T(8,128)(2,1)} copy(bf16[256,32,256]{0,2,1:T(8,128)(2,1)} %get-tuple-element.4) | data formatting | bytes 8388608 | tf_op jit(solution)/shard_map/slice | solution.py:24
  115.7 8.2 %copy.37 = bf16[256,32,256]{2,1,0:T(8,128)(2,1)} copy(bf16[256,32,256]{0,2,1:T(8,128)(2,1)} %get-tuple-element.3) | data formatting | bytes 8388608 | tf_op jit(solution)/shard_map/slice | solution.py:24
  124.0 3.6 fusion.92
  138.6 1.4 convolution_add_fusion.2
  144.2 4.9 copy.38
  150.3 3.5 collective-permute-start.6
  153.8 1.9 collective-permute-start.7
  155.7 3.1 collective-permute-done.7
  160.7 4.7 collective-permute-start.9
  166.8 4.2 pad_maximum_fusion.7
  174.5 20.6 %reduce-scatter.2.cloned.1.call-done = bf16[64,32,256]{2,0,1:T(8,128)(2,1)} async-done(((bf16[256,32,256]{2,0,1:T(8,128)(2,1)}), bf16[64,32,256]{2,0,1:T(8,128)(2,1)}) %reduce-scatter.2.cloned.1.call-update) | async-done | bytes 1048592 | tf_op jit(solution)/shard_map/reduce_scatter | solution.py:82
  195.1 3.7 fusion.25
  199.0 2.6 collective-permute-start.3
  201.6 3.0 collective-permute-start.2
  204.6 2.5 convolution_bitcast_fusion.5
  207.1 1.6 copy.43
  208.7 1.4 collective-permute-start.5
  210.1 4.2 collective-permute-start.4
  218.2 1.6 copy.46
  220.6 2.9 fusion.146
  224.1 1.6 copy.41
  225.6 1.6 copy.42
  227.2 1.6 copy.44
  232.5 1.5 convolution_bitcast_fusion.7
  240.8 5.9 %fusion.52 = bf16[1,256,256]{2,1,0:T(8,128)(2,1)S(1)} fusion(bf16[256,32,256]{2,0,1:T(8,128)(2,1)} %all-gather.2.cloned.1.call-done, bf16[258,34,256]{0,2,1:T(8,128)(2,1)} %fusion.6), kind=kOutput, calls=%fused_computation.97 | convolution fusion | flops 1073807360 | bytes 8519680 | tf_op jit(solution)/shard_map/dot_general | solution.py:59
  246.8 4.7 fusion.53
  251.5 1.8 fusion.54
  254.6 1.5 fusion.56
  263.4 3.2 pad_maximum_fusion.2
  266.6 1.7 convolution_add_fusion.20
  270.2 1.7 convolution_add_fusion.17
  275.4 1.4 fusion.17
  276.8 65.8 %all-reduce.4.cloned.1.call-done = bf16[3,3,256,256]{3,2,1,0:T(8,128)(2,1)} async-done(((bf16[3,3,256,256]{3,2,1,0:T(8,128)(2,1)}), bf16[3,3,256,256]{3,2,1,0:T(8,128)(2,1)}) %all-reduce.4.cloned.1.call-update) | async-done | bytes 1179664 | tf_op jit(solution)/shard_map/psum | solution.py:101
  342.6 2.9 convert_element_type.34
  345.5 137.1 %all-reduce.6.cloned.1.call-done = f32[3,3,256,256]{3,2,1,0:T(8,128)} async-done(((f32[3,3,256,256]{3,2,1,0:T(8,128)}), f32[3,3,256,256]{3,2,1,0:T(8,128)}) %all-reduce.6.cloned.1.call-update) | async-done | bytes 2359312 | tf_op jit(solution)/shard_map/psum | solution.py:102
  482.6 3.2 copy.85
  (125 shorter events, 56.1 us)
Async XLA Ops:
  7.2 187.9 %reduce-scatter.2.cloned.1.call-start = ((), (), s32[]{:S(2)}) async-start(), calls=%async_computation.1 | async-start | bytes 5242880 | tf_op jit(solution)/shard_map/reduce_scatter | solution.py:82
  15.8 7.2 %collective-permute-start.1 = (bf16[256,1,256]{0,2,1:T(8,128)(2,1)S(1)}, bf16[256,1,256]{0,2,1:T(8,128)(2,1)S(1)}, u32[]{:S(2)}, u32[]{:S(2)}) collective-permute-start(bf16[256,1,256]{0,2,1:T(8,128)(2,1)S(1)} %get-tuple-element.12), channel_id=1, source_target_pairs={{1,0},{2,1},{3,2},{4,3},{5,4},{6,5},{7,6},{9,8},{10,9},{11,10},{12... | collective-permute-start | bytes 393224 | tf_op jit(solution)/shard_map/ppermute | solution.py:15
  17.1 9.6 %collective-permute-start = (bf16[256,1,256]{0,2,1:T(8,128)(2,1)S(1)}, bf16[256,1,256]{0,2,1:T(8,128)(2,1)S(1)}, u32[]{:S(2)}, u32[]{:S(2)}) collective-permute-start(bf16[256,1,256]{0,2,1:T(8,128)(2,1)S(1)} %get-tuple-element.11), channel_id=1, source_target_pairs={{0,1},{1,2},{2,3},{3,4},{4,5},{5,6},{6,7},{8,9},{9,10},{10,11},{11... | collective-permute-start | bytes 393224 | tf_op jit(solution)/shard_map/ppermute | solution.py:14
  22.9 55.2 %copy-start.19 = (bf16[256,1,256]{0,2,1:T(8,128)(2,1)}, bf16[256,1,256]{0,2,1:T(8,128)(2,1)S(1)}, u32[]{:S(2)}) copy-start(bf16[256,1,256]{0,2,1:T(8,128)(2,1)S(1)} %collective-permute-done.1) | copy-start | bytes 393220
  26.6 51.5 %copy-start.21 = (bf16[256,1,256]{0,2,1:T(8,128)(2,1)}, bf16[256,1,256]{0,2,1:T(8,128)(2,1)S(1)}, u32[]{:S(2)}) copy-start(bf16[256,1,256]{0,2,1:T(8,128)(2,1)S(1)} %collective-permute-done) | copy-start | bytes 393220
  115.7 8.2 %copy-start.18 = (bf16[3,3,256,256]{3,2,1,0:T(8,128)(2,1)S(1)}, bf16[3,3,256,256]{3,2,1,0:T(8,128)(2,1)}, u32[]{:S(2)}) copy-start(bf16[3,3,256,256]{3,2,1,0:T(8,128)(2,1)} %param.5) | copy-start | bytes 3538948
  124.0 3.6 copy-start.7
  127.6 2.2 copy-start.5
  129.8 2.2 copy-start.8
  132.0 2.2 copy-start.2
  134.2 2.2 copy-start.6
  136.4 2.2 copy-start.4
  138.6 2.2 copy-start.3
  140.7 2.2 copy-start.1
  149.0 1.2 copy-start.11
  149.1 91.7 %all-gather.2.cloned.1.call-start = ((), (), s32[]{:S(2)}) async-start(), calls=%async_computation.2 | async-start | bytes 5242880 | tf_op jit(solution)/shard_map/all_gather | solution.py:97
  150.3 5.5 %collective-permute-start.6 = (bf16[1,32,256]{2,1,0:T(8,128)(2,1)S(1)}, bf16[1,32,256]{2,1,0:T(8,128)(2,1)S(1)}, u32[]{:S(2)}, u32[]{:S(2)}) collective-permute-start(bf16[1,32,256]{2,1,0:T(8,128)(2,1)S(1)} %get-tuple-element.40), channel_id=1, source_target_pairs={{0,8},{8,16},{16,24},{1,9},{9,17},{17,25},{2,10},{10,18},{18,26},{... | collective-permute-start | bytes 49160 | tf_op jit(solution)/shard_map/ppermute | solution.py:14
  153.8 5.1 %collective-permute-start.7 = (bf16[1,32,256]{2,1,0:T(8,128)(2,1)S(1)}, bf16[1,32,256]{2,1,0:T(8,128)(2,1)S(1)}, u32[]{:S(2)}, u32[]{:S(2)}) collective-permute-start(bf16[1,32,256]{2,1,0:T(8,128)(2,1)S(1)} %get-tuple-element.39), channel_id=1, source_target_pairs={{8,0},{16,8},{24,16},{9,1},{17,9},{25,17},{10,2},{18,10},{26,18},{... | collective-permute-start | bytes 49160 | tf_op jit(solution)/shard_map/ppermute | solution.py:15
  155.7 9.7 %copy-start.9 = (bf16[3,3,256,256]{3,2,1,0:T(8,128)(2,1)S(1)}, bf16[3,3,256,256]{3,2,1,0:T(8,128)(2,1)}, u32[]{:S(2)}) copy-start(bf16[3,3,256,256]{3,2,1,0:T(8,128)(2,1)} %param.6) | copy-start | bytes 3538948
  159.4 7.0 %collective-permute-start.8 = (bf16[66,1,256]{2,1,0:T(2,128)(2,1)S(1)}, bf16[66,1,256]{2,1,0:T(2,128)(2,1)S(1)}, u32[]{:S(2)}, u32[]{:S(2)}) collective-permute-start(bf16[66,1,256]{2,1,0:T(2,128)(2,1)S(1)} %get-tuple-element.32), channel_id=1, source_target_pairs={{1,0},{2,1},{3,2},{4,3},{5,4},{6,5},{7,6},{9,8},{10,9},{11,10},{12... | collective-permute-start | bytes 101384 | tf_op jit(solution)/shard_map/ppermute | solution.py:15
  160.7 6.1 %collective-permute-start.9 = (bf16[66,1,256]{2,1,0:T(2,128)(2,1)S(1)}, bf16[66,1,256]{2,1,0:T(2,128)(2,1)S(1)}, u32[]{:S(2)}, u32[]{:S(2)}) collective-permute-start(bf16[66,1,256]{2,1,0:T(2,128)(2,1)S(1)} %get-tuple-element.33), channel_id=1, source_target_pairs={{0,1},{1,2},{2,3},{3,4},{4,5},{5,6},{6,7},{8,9},{9,10},{10,11},{11... | collective-permute-start | bytes 101384 | tf_op jit(solution)/shard_map/ppermute | solution.py:14
  198.9 143.7 %all-reduce.4.cloned.1.call-start = ((), (), s32[]{:S(2)}) async-start(), calls=%async_computation.3 | async-start | bytes 2359296 | tf_op jit(solution)/shard_map/psum | solution.py:101
  199.0 9.7 %collective-permute-start.3 = (bf16[1,32,256]{2,0,1:T(2,128)(2,1)S(1)}, bf16[1,32,256]{2,0,1:T(2,128)(2,1)S(1)}, u32[]{:S(2)}, u32[]{:S(2)}) collective-permute-start(bf16[1,32,256]{2,0,1:T(2,128)(2,1)S(1)} %get-tuple-element.44), channel_id=1, source_target_pairs={{8,0},{16,8},{24,16},{9,1},{17,9},{25,17},{10,2},{18,10},{26,18},{... | collective-permute-start | bytes 49160 | tf_op jit(solution)/shard_map/ppermute | solution.py:15
  201.6 7.1 %collective-permute-start.2 = (bf16[1,32,256]{2,0,1:T(2,128)(2,1)S(1)}, bf16[1,32,256]{2,0,1:T(2,128)(2,1)S(1)}, u32[]{:S(2)}, u32[]{:S(2)}) collective-permute-start(bf16[1,32,256]{2,0,1:T(2,128)(2,1)S(1)} %get-tuple-element.43), channel_id=1, source_target_pairs={{0,8},{8,16},{16,24},{1,9},{9,17},{17,25},{2,10},{10,18},{18,26},{... | collective-permute-start | bytes 49160 | tf_op jit(solution)/shard_map/ppermute | solution.py:14
  208.7 6.4 %copy-start.12 = (bf16[64,32,256]{2,1,0:T(8,128)(2,1)S(1)}, bf16[64,32,256]{2,1,0:T(8,128)(2,1)}, u32[]{:S(2)}) copy-start(bf16[64,32,256]{2,1,0:T(8,128)(2,1)} %param.7) | copy-start | bytes 3145732
  208.7 11.1 %collective-permute-start.5 = (bf16[66,1,256]{2,0,1:T(8,128)(2,1)S(1)}, bf16[66,1,256]{2,0,1:T(8,128)(2,1)S(1)}, u32[]{:S(2)}, u32[]{:S(2)}) collective-permute-start(bf16[66,1,256]{2,0,1:T(8,128)(2,1)S(1)} %get-tuple-element.27), channel_id=1, source_target_pairs={{1,0},{2,1},{3,2},{4,3},{5,4},{6,5},{7,6},{9,8},{10,9},{11,10},{12... | collective-permute-start | bytes 101384 | tf_op jit(solution)/shard_map/ppermute | solution.py:15
  210.1 9.6 %collective-permute-start.4 = (bf16[66,1,256]{2,0,1:T(8,128)(2,1)S(1)}, bf16[66,1,256]{2,0,1:T(8,128)(2,1)S(1)}, u32[]{:S(2)}, u32[]{:S(2)}) collective-permute-start(bf16[66,1,256]{2,0,1:T(8,128)(2,1)S(1)} %get-tuple-element.28), channel_id=1, source_target_pairs={{0,1},{1,2},{2,3},{3,4},{4,5},{5,6},{6,7},{8,9},{9,10},{10,11},{11... | collective-permute-start | bytes 101384 | tf_op jit(solution)/shard_map/ppermute | solution.py:14
  238.1 1.8 copy-start.10
  240.8 6.0 %copy-start.23 = (bf16[256,32,256]{2,0,1:T(8,128)(2,1)S(1)}, bf16[256,32,256]{2,0,1:T(8,128)(2,1)}, u32[]{:S(2)}) copy-start(bf16[256,32,256]{2,0,1:T(8,128)(2,1)} %all-gather.2.cloned.1.call-done) | copy-start | bytes 12582916
  240.8 10.7 %slice-start = ((s8[6684672]{0:T(1024)(128)(4,1)}), s8[4194304]{0:T(1024)(128)(4,1)S(1)}, s32[]{:S(2)}) async-start(s8[6684672]{0:T(1024)(128)(4,1)} %bitcast.255), calls=%async_computation.5 | async-start | bytes 8388608
  246.8 4.8 slice-start.1
  256.2 2.2 copy-start
  256.2 2.2 copy-start.20
  259.6 1.3 copy-start.22
  263.4 219.2 %all-reduce.6.cloned.1.call-start = ((), (), s32[]{:S(2)}) async-start(), calls=%async_computation.4 | async-start | bytes 4718592 | tf_op jit(solution)/shard_map/psum | solution.py:102
  266.6 1.8 copy-start.17
  268.4 1.4 copy-start.15
  270.2 1.8 copy-start.14
  271.9 1.2 copy-start.13
  273.8 1.2 copy-start.16
Sparse Core Ops, SparseCore 0:
  149.2 45.8 reduce-scatter.1
  199.0 34.8 all-gather.1
  263.5 79.0 all-reduce.3
  348.6 134.0 all-reduce.5
where the time goes:
time: 503 us; the launch traced here: 493 us
  waiting for transfers between devices  232 us (46%)
  local copies, waits for them, and re-layouts  125 us (25%)
  matrix products  59.3 us (12%)
  other arithmetic  33.4 us (7%)
  starting transfers between devices  28.6 us (6%)
  between operations  14.9 us (3%)
    psum x1, waiting for transfers between devices, body(): grad_second = lax.psum(second_part, ('freq', 'sky'))  137 us
    slice x18, local copies, waits for them, and re-layouts, conv_taps(): padded[tap_col:tap_col + col_count, tap_row:tap_row + row_count]  95.1 us
    psum x1, waiting for transfers between devices, body(): lax.psum(first_part.astype(jnp.bfloat16), 'sky').astype(jnp.float32)  65.8 us
    dot_general x18, matrix products, kernel_grad(): lax.dot_general(piece, flat, (((0,), (0,)), ((), ())), preferred_element_...  33.5 us
    unnamed x55, local copies, waits for them, and re-layouts  21.9 us
    dot_general x18, matrix products, conv_taps(): jnp.dot(piece, kernel[tap_col, tap_row], preferred_element_type=jnp.float32)  21.4 us
    reduce_scatter x1, waiting for transfers between devices, body(): lax.psum_scatter(conv_taps(slab, weight_first, strip * lax.axis_size('fre...  20.6 us
    ppermute x5, starting transfers between devices, with_halo(): before = lax.ppermute(last, axis, up)  20 us
  transfers between devices with their start and end apart: 14, of which 7 were waited for; matrix products, arithmetic and copies ran while one was open for 11% of the time, Pallas kernels for 0%

commit v1 on v0

v1 whole, which is shorter than its diff:
```python
import functools

import jax
import jax.numpy as jnp
from jax import lax
from jax.experimental import pallas as pl
from jax.experimental.pallas import tpu as pltpu
from jax.sharding import PartitionSpec as P

MESH = pl.DeviceIdType.MESH
VMEM_LIMIT = 56 * 1024 * 1024
BLOCK = 16


def build_shifts(x_ref, top_ref, bot_ref, shifts, pad):
    count, rows, chans = x_ref.shape
    if pad:
        zero = jnp.zeros((1, rows, chans), shifts.dtype)
        for q in range(3):
            shifts[q, 0:1] = zero
            shifts[q, count + 1 : count + 2] = zero
    step = 8 if count % 8 == 0 else 2
    row = lax.broadcasted_iota(jnp.int32, (step, rows, chans), 1)

    def one(i, carry):
        c = i * step
        x = x_ref[pl.ds(c, step)]
        shifts[1, pl.ds(c + pad, step)] = x
        wide = x.astype(jnp.float32)
        top = jnp.broadcast_to(top_ref[pl.ds(c, step)], wide.shape)
        bot = jnp.broadcast_to(bot_ref[pl.ds(c, step)], wide.shape)
        up = jnp.where(row == 0, top, pltpu.roll(wide, 1, 1))
        down = jnp.where(row == rows - 1, bot, pltpu.roll(wide, rows - 1, 1))
        shifts[0, pl.ds(c + pad, step)] = up.astype(shifts.dtype)
        shifts[2, pl.ds(c + pad, step)] = down.astype(shifts.dtype)
        return carry

    lax.fori_loop(0, count // step, one, 0)


def conv_kernel(pad, x_ref, top_ref, bot_ref, w_ref, out_ref, shifts):
    build_shifts(x_ref, top_ref, bot_ref, shifts, pad)
    rows, chans = x_ref.shape[1:]
    count = shifts.shape[1] - 2

    def one(i, carry):
        c = i * BLOCK
        total = None
        for q in range(3):
            for p in range(3):
                piece = shifts[q, pl.ds(c + p, BLOCK)].reshape(BLOCK * rows, chans)
                term = jnp.dot(piece, w_ref[p, q], preferred_element_type=jnp.float32)
                total = term if total is None else total + term
        out_ref[pl.ds(c * rows, BLOCK * rows)] = total.astype(out_ref.dtype)
        return carry

    lax.fori_loop(0, count // BLOCK, one, 0)


def conv(x, top, bot, w, pad, dtype):
    count = x.shape[0] - (0 if pad else 2)
    rows, chans = x.shape[1:]
    return pl.pallas_call(
        functools.partial(conv_kernel, pad),
        out_shape=jax.ShapeDtypeStruct((count * rows, w.shape[3]), dtype),
        in_specs=[pl.BlockSpec(memory_space=pltpu.VMEM)] * 4,
        out_specs=pl.BlockSpec(memory_space=pltpu.VMEM),
        scratch_shapes=[pltpu.VMEM((3, count + 2, rows, chans), jnp.bfloat16)],
        compiler_params=pltpu.CompilerParams(vmem_limit_bytes=VMEM_LIMIT),
        cost_estimate=pl.CostEstimate(
            flops=18 * count * rows * chans * w.shape[3],
            bytes_accessed=4 * x.size + 2 * w.size,
            transcendentals=0,
        ),
    )(x, top[:, None, :].astype(jnp.float32), bot[:, None, :].astype(jnp.float32), w)


def grad_kernel(pad, x_ref, top_ref, bot_ref, d_ref, out_ref, shifts, flipped, sums):
    build_shifts(x_ref, top_ref, bot_ref, shifts, pad)
    rows, chans = x_ref.shape[1:]
    count = shifts.shape[1] - 2
    cols = min(32, count)
    span = cols * rows

    def one(i, carry):
        c = i * cols
        for k in range(span // 256):
            block = d_ref[pl.ds(c * rows + k * 256, 256)]
            flipped[:, k * 256 : (k + 1) * 256] = block.T
        for q in range(3):
            for p in range(3):
                piece = shifts[q, pl.ds(c + p, cols)].reshape(span, chans)
                sums[p, q] += jnp.dot(flipped[...], piece, preferred_element_type=jnp.float32)
        return carry

    sums[...] = jnp.zeros_like(sums)
    lax.fori_loop(0, count // cols, one, 0)
    for p in range(3):
        for q in range(3):
            out_ref[p, q] = sums[p, q].T


def kernel_grad(x, top, bot, d, pad):
    count = x.shape[0] - (0 if pad else 2)
    rows, chans = x.shape[1:]
    outs = d.shape[1]
    return pl.pallas_call(
        functools.partial(grad_kernel, pad),
        out_shape=jax.ShapeDtypeStruct((3, 3, chans, outs), jnp.float32),
        in_specs=[pl.BlockSpec(memory_space=pltpu.VMEM)] * 4,
        out_specs=pl.BlockSpec(memory_space=pltpu.VMEM),
        scratch_shapes=[
            pltpu.VMEM((3, count + 2, rows, chans), jnp.bfloat16),
            pltpu.VMEM((outs, min(32, count) * rows), jnp.bfloat16),
            pltpu.VMEM((3, 3, outs, chans), jnp.float32),
        ],
        compiler_params=pltpu.CompilerParams(vmem_limit_bytes=VMEM_LIMIT),
        cost_estimate=pl.CostEstimate(
            flops=18 * count * rows * chans * outs,
            bytes_accessed=4 * x.size,
            transcendentals=0,
        ),
    )(x, top[:, None, :].astype(jnp.float32), bot[:, None, :].astype(jnp.float32), d)


def sum_kernel(axis, count, g_ref, out_ref, mine, landed, full, send, recv, send2, recv2):
    me = lax.axis_index(axis)
    chunk = g_ref.shape[0] // count
    barrier = pltpu.get_barrier_semaphore()
    for k in range(1, count):
        pl.semaphore_signal(
            barrier, inc=1, device_id={axis: lax.rem(me + k, count)}, device_id_type=MESH
        )
    mine[...] = g_ref[...].astype(mine.dtype)
    pl.semaphore_wait(barrier, count - 1)

    def rows_of(i):
        return pl.ds(pl.multiple_of(i * chunk, 16), chunk)

    def scatter(k):
        peer = lax.rem(me + k, count)
        return pltpu.make_async_remote_copy(
            src_ref=mine.at[rows_of(peer)],
            dst_ref=landed.at[k - 1],
            send_sem=send.at[k - 1],
            recv_sem=recv.at[k - 1],
            device_id={axis: peer},
            device_id_type=MESH,
        )

    def gather(k):
        return pltpu.make_async_remote_copy(
            src_ref=full.at[rows_of(me)],
            dst_ref=full.at[rows_of(me)],
            send_sem=send2.at[k - 1],
            recv_sem=recv2.at[k - 1],
            device_id={axis: lax.rem(me + k, count)},
            device_id_type=MESH,
        )

    first = [scatter(k) for k in range(1, count)]
    for copy in first:
        copy.start()
    total = g_ref[rows_of(me)]
    for k in range(1, count):
        first[k - 1].wait_recv()
        total = total + landed[k - 1].astype(jnp.float32)
    full[rows_of(me)] = total.astype(full.dtype)
    second = [gather(k) for k in range(1, count)]
    for copy in second:
        copy.start()
    out_ref[rows_of(me)] = full[rows_of(me)].astype(out_ref.dtype)
    for k in range(1, count):
        second[k - 1].wait_recv()
        source = rows_of(lax.rem(me + count - k, count))
        out_ref[source] = full[source].astype(out_ref.dtype)
    for copy in first + second:
        copy.wait_send()


def sum_over(g, axis):
    count = lax.axis_size(axis)
    given, cols = g.shape
    rows = -(-given // (16 * count)) * 16 * count
    if rows != given:
        g = jnp.pad(g, ((0, rows - given), (0, 0)))
    return pl.pallas_call(
        functools.partial(sum_kernel, axis, count),
        out_shape=jax.ShapeDtypeStruct((rows, cols), jnp.float32),
        in_specs=[pl.BlockSpec(memory_space=pltpu.VMEM)],
        out_specs=pl.BlockSpec(memory_space=pltpu.VMEM),
        scratch_shapes=[
            pltpu.VMEM((rows, cols), jnp.bfloat16),
            pltpu.VMEM((count - 1, rows // count, cols), jnp.bfloat16),
            pltpu.VMEM((rows, cols), jnp.bfloat16),
        ]
        + [pltpu.SemaphoreType.DMA((count - 1,))] * 4,
        compiler_params=pltpu.CompilerParams(
            collective_id=0, has_side_effects=True, vmem_limit_bytes=VMEM_LIMIT
        ),
        cost_estimate=pl.CostEstimate(flops=0, bytes_accessed=40 * g.size, transcendentals=0),
    )(g)[:given]


def neighbours(first, last, axis):
    count = lax.axis_size(axis)
    up = [(i, i + 1) for i in range(count - 1)]
    down = [(j, i) for i, j in up]
    return lax.ppermute(last, axis, up), lax.ppermute(first, axis, down)


def with_columns(x):
    before, after = neighbours(x[:1], x[-1:], "freq")
    return jnp.concatenate([before, x, after], axis=0)


def silu_slope(pre):
    sigma = jax.nn.sigmoid(pre)
    return sigma * (1.0 + pre * (1.0 - sigma))


def body(sky_cube, weight_first, weight_second, cotangent):
    strip, rows, chans = cotangent.shape
    top, bot = neighbours(sky_cube[:, 0], sky_cube[:, -1], "sky")
    partial = conv(sky_cube, top, bot, weight_first, 1, jnp.bfloat16)
    pre = lax.psum_scatter(partial, "freq", scatter_dimension=0, tiled=True)
    pre = pre.astype(jnp.float32)
    cot_pad = with_columns(cotangent)
    cot_top, cot_bot = neighbours(cot_pad[:, 0], cot_pad[:, -1], "sky")
    weight_back = jnp.transpose(weight_second[::-1, ::-1], (0, 1, 3, 2))
    back = conv(cot_pad, cot_top, cot_bot, weight_back, 0, jnp.float32)
    delta = (back * silu_slope(pre)).astype(jnp.bfloat16)
    whole = lax.all_gather(delta, "freq", axis=0, tiled=True)
    hidden = jax.nn.silu(pre).astype(jnp.bfloat16).reshape(strip, rows, chans)
    hidden_pad = with_columns(hidden)
    hid_top, hid_bot = neighbours(hidden_pad[:, 0], hidden_pad[:, -1], "sky")
    second = kernel_grad(hidden_pad, hid_top, hid_bot, cotangent.reshape(strip * rows, -1), 0)
    features = conv(hidden_pad, hid_top, hid_bot, weight_second, 0, jnp.bfloat16)
    grad_second = lax.psum(second.astype(jnp.bfloat16), ("freq", "sky")).astype(jnp.float32)
    first = kernel_grad(sky_cube, top, bot, whole, 1)
    grad_first = sum_over(first.reshape(-1, first.shape[3]), "sky").reshape(first.shape)
    return (features.reshape(strip, rows, -1), grad_first, grad_second)


def solution(mesh):
    return jax.shard_map(
        body,
        mesh=mesh,
        in_specs=(P(None, "sky", "freq"), P(None, None, "freq", None), P(), P("freq", "sky", None)),
        out_specs=(P("freq", "sky", None), P(None, None, "freq", None), P()),
        check_vma=False,
    )
```

time: 503 us -> 377 us (0.75)
  Pallas kernels: 0 us -> 113 us
  local copies, waits for them, and re-layouts: 125 us -> 16.4 us
  matrix products: 59.3 us -> 0 us
  waiting for transfers between devices: 232 us -> 188 us
  other arithmetic: 33.4 us -> 10.8 us
    pallas_call x0 -> x6, Pallas kernels: none -> 113 us  [the longest x1 53.8 us: sum_over(): pl.pallas_call(functools.partial(sum_kernel, axis, count), out_shape=jax....]
    slice x22 -> x5, local copies, waits for them, and re-layouts: 96.3 us -> 2.08 us  [the longest x1 1.97 us: body(): top, bot = neighbours(sky_cube[:, 0], sky_cube[:, -1], 'sky')]
    psum x2 -> x1, waiting for transfers between devices: 203 us -> 126 us  [body(): lax.psum(second.astype(jnp.bfloat16), ('freq', 'sky')).astype(jnp.float32)]
    dot_general x45 -> x0, matrix products: 59.3 us -> none  [the longest x18 33.5 us: kernel_grad(): lax.dot_general(piece, flat, (((0,), (0,)), ((), ())), preferred_element_...]
    all_gather x1, waiting for transfers between devices: 0.02 us -> 33.5 us  [body(): whole = lax.all_gather(delta, 'freq', axis=0, tiled=True)]
    unnamed x55 -> x9, local copies, waits for them, and re-layouts: 21.9 us -> 5.72 us
    concatenate x6 -> x2, other arithmetic: 14.1 us -> 1.42 us  [with_columns(): return jnp.concatenate([before, x, after], axis=0)]
    another operation x6 -> x0, other arithmetic: 6.75 us -> none  [kernel_grad(): return jnp.stack(rows_out)]
  transfers between devices with their start and end apart: 14 -> 13, of which waited for: 7 -> 9; matrix products, arithmetic and copies ran while one was open for 11% -> 3% of each run, Pallas kernels for 0% -> 4%
where the time goes in v1:
time: 377 us; the launch traced here: 370 us
  waiting for transfers between devices  188 us (50%)
  Pallas kernels  113 us (30%)
  starting transfers between devices  27.9 us (7%)
  local copies, waits for them, and re-layouts  16.4 us (4%)
  between operations  14 us (4%)
  other arithmetic  10.8 us (3%)
    psum x1, waiting for transfers between devices, body(): lax.psum(second.astype(jnp.bfloat16), ('freq', 'sky')).astype(jnp.float32)  126 us
    pallas_call x1, Pallas kernels, sum_over(): pl.pallas_call(functools.partial(sum_kernel, axis, count), out_shape=jax....  53.8 us
    all_gather x1, waiting for transfers between devices, body(): whole = lax.all_gather(delta, 'freq', axis=0, tiled=True)  33.5 us
    pallas_call x3, Pallas kernels, conv(): pl.pallas_call(functools.partial(conv_kernel, pad), out_shape=jax.ShapeDt...  32.1 us
    ppermute x10, starting transfers between devices, neighbours(): return (lax.ppermute(last, axis, up), lax.ppermute(first, axis, down))  27.6 us
    pallas_call x2, Pallas kernels, kernel_grad(): pl.pallas_call(functools.partial(grad_kernel, pad), out_shape=jax.ShapeDt...  26.6 us
    reduce_scatter x1, waiting for transfers between devices, body(): pre = lax.psum_scatter(partial, 'freq', scatter_dimension=0, tiled=True)  15.5 us
    ppermute x10, waiting for transfers between devices, neighbours(): return (lax.ppermute(last, axis, up), lax.ppermute(first, axis, down))  13 us
  transfers between devices with their start and end apart: 13, of which 9 were waited for; matrix products, arithmetic and copies ran while one was open for 3% of the time, Pallas kernels for 4%

profile of v1, /device:TPU:1, one launch (start us, length us, event | category | flops | bytes accessed | tf_op | source)
XLA Modules:
  0.0 369.6 jit_solution(18119052771589276019)
XLA Ops:
  7.2 2.0 fusion.8
  9.2 4.0 %collective-permute-start = (bf16[256,256]{1,0:T(8,128)(2,1)S(1)}, bf16[256,256]{1,0:T(8,128)(2,1)S(1)}, u32[]{:S(2)}, u32[]{:S(2)}) collective-permute-start(bf16[256,256]{1,0:T(8,128)(2,1)S(1)} %bitcast.35), channel_id=1, source_target_pairs={{0,1},{1,2},{2,3},{3,4},{4,5},{5,6},{6,7},{8,9},{9,10},{10,11},{11... | collective-permute-start | bytes 393224 | tf_op jit(solution)/shard_map/ppermute | solution.py:209
  13.2 1.3 collective-permute-start.1
  14.5 0.8 collective-permute-done
  15.3 0.8 reshape.40.top_ref
  16.1 2.8 collective-permute-done.1
  18.9 0.9 reshape.41.bot_ref
  19.8 19.2 %shard_map.67 = bf16[8192,256]{1,0:T(8,128)(2,1)} custom-call(bf16[256,32,256]{2,1,0:T(8,128)(2,1)} %x_ref.3, f32[256,1,256]{2,1,0:T(1,128)} %reshape.40.top_ref, f32[256,1,256]{2,1,0:T(1,128)} %reshape.41.bot_ref, bf16[3,3,256,256]{3,2,1,0:T(8,128)(2,1)} %w_ref.2), custom_call_target="tpu_custom_call" | custom-call | flops 9663676416 | bytes 9568256 | tf_op jit(solution)/shard_map/pallas_call | solution.py:63
  39.0 1.1 copy-done.1
  40.2 0.6 copy.41
  40.7 0.1 fusion.9
  40.8 5.1 %collective-permute-start.6 = (bf16[1,32,256]{2,0,1:T(2,128)(2,1)S(1)}, bf16[1,32,256]{2,0,1:T(2,128)(2,1)S(1)}, u32[]{:S(2)}, u32[]{:S(2)}) collective-permute-start(bf16[1,32,256]{2,0,1:T(2,128)(2,1)S(1)} %get-tuple-element.11), channel_id=1, source_target_pairs={{0,8},{8,16},{16,24},{1,9},{9,17},{17,25},{2,10},{10,18},{18,26},{... | collective-permute-start | bytes 49160 | tf_op jit(solution)/shard_map/ppermute | solution.py:209
  46.0 1.9 collective-permute-start.7
  47.9 0.7 copy.44
  48.6 2.5 collective-permute-done.7
  51.2 0.7 pad_maximum_fusion.1
  51.9 4.1 %collective-permute-start.8 = (bf16[66,256]{1,0:T(8,128)(2,1)S(1)}, bf16[66,256]{1,0:T(8,128)(2,1)S(1)}, u32[]{:S(2)}, u32[]{:S(2)}) collective-permute-start(bf16[66,256]{1,0:T(8,128)(2,1)S(1)} %get-tuple-element.6), channel_id=1, source_target_pairs={{0,1},{1,2},{2,3},{3,4},{4,5},{5,6},{6,7},{8,9},{9,10},{10,11},{11... | collective-permute-start | bytes 101384 | tf_op jit(solution)/shard_map/ppermute | solution.py:209
  56.0 1.1 reverse_bitcast_fusion.w_ref
  57.1 1.2 copy.45.x_ref
  58.3 1.3 collective-permute-start.9
  59.6 0.7 copy.46.top_ref
  60.3 3.1 collective-permute-done.9
  63.4 0.7 reshape.45.bot_ref
  64.1 6.7 %shard_map.69 = f32[2048,256]{1,0:T(8,128)} custom-call(bf16[66,32,256]{2,1,0:T(8,128)(2,1)} %copy.45.x_ref, f32[66,1,256]{2,1,0:T(1,128)} %copy.46.top_ref, f32[66,1,256]{2,1,0:T(1,128)} %reshape.45.bot_ref, bf16[3,3,256,256]{3,2,1,0:T(8,128)(2,1)} %reverse_bitcast_fusion.w_ref), custom_call_target="tpu_custom_call" | custom-call | flops 2415919104 | bytes 3342336 | tf_op jit(solution)/shard_map/pallas_call | solution.py:63
  70.7 15.5 %reduce-scatter.2.cloned.1.call-done = bf16[2048,256]{1,0:T(8,128)(2,1)} async-done(((bf16[8192,256]{1,0:T(8,128)(2,1)}), bf16[2048,256]{1,0:T(8,128)(2,1)}) %reduce-scatter.2.cloned.1.call-update) | async-done | bytes 1048592 | tf_op jit(solution)/shard_map/reduce_scatter | solution.py:226
  86.3 3.7 fusion.7
  90.0 2.6 collective-permute-start.3
  92.6 3.0 collective-permute-start.2
  95.6 0.6 copy.38
  96.2 0.4 collective-permute-done.2
  96.6 0.7 pad_maximum_fusion
  97.3 3.1 collective-permute-start.4
  100.4 1.3 copy.39.x_ref
  101.7 1.3 collective-permute-start.5
  103.0 0.7 copy.40.top_ref
  103.7 3.3 collective-permute-done.5
  107.0 0.7 reshape.43.bot_ref
  107.7 7.3 %shard_map.72 = f32[3,3,256,256]{3,2,1,0:T(8,128)} custom-call(bf16[66,32,256]{2,1,0:T(8,128)(2,1)} %copy.39.x_ref, f32[66,1,256]{2,1,0:T(1,128)} %copy.40.top_ref, f32[66,1,256]{2,1,0:T(1,128)} %reshape.43.bot_ref, bf16[2048,256]{1,0:T(8,128)(2,1)} %bitcast.34), custom_call_target="tpu_custom_call" | custom-call | flops 2415919104 | bytes 2162688 | tf_op jit(solution)/shard_map/pallas_call | solution.py:107
  115.0 2.8 convert_element_type.64
  117.8 0.2 all-gather.2.cloned.1.call-start
  118.0 0.5 all-gather.2.cloned.1.call-update
  118.5 6.3 %shard_map.68 = bf16[2048,256]{1,0:T(8,128)(2,1)} custom-call(bf16[66,32,256]{2,1,0:T(8,128)(2,1)} %copy.39.x_ref, f32[66,1,256]{2,1,0:T(1,128)} %copy.40.top_ref, f32[66,1,256]{2,1,0:T(1,128)} %reshape.43.bot_ref, bf16[3,3,256,256]{3,2,1,0:T(8,128)(2,1)} %w_ref.3), custom_call_target="tpu_custom_call" | custom-call | flops 2415919104 | bytes 3342336 | tf_op jit(solution)/shard_map/pallas_call | solution.py:63
  124.9 125.5 %all-reduce.2.cloned.1.call-done = bf16[3,3,256,256]{3,2,1,0:T(8,128)(2,1)} async-done(((bf16[3,3,256,256]{3,2,1,0:T(8,128)(2,1)}), bf16[3,3,256,256]{3,2,1,0:T(8,128)(2,1)}) %all-reduce.2.cloned.1.call-update) | async-done | bytes 1179664 | tf_op jit(solution)/shard_map/psum | solution.py:239
  250.4 2.9 convert_element_type.65
  253.3 33.5 %all-gather.2.cloned.1.call-done.d_ref = bf16[8192,256]{1,0:T(8,128)(2,1)} async-done(((bf16[2048,256]{1,0:T(8,128)(2,1)}), bf16[8192,256]{1,0:T(8,128)(2,1)}) %all-gather.2.cloned.1.call-update) | async-done | bytes 4194320 | tf_op jit(solution)/shard_map/all_gather | solution.py:233
  286.7 19.4 %shard_map.70 = f32[3,3,256,256]{3,2,1,0:T(8,128)} custom-call(bf16[256,32,256]{2,1,0:T(8,128)(2,1)} %x_ref.3, f32[256,1,256]{2,1,0:T(1,128)} %reshape.40.top_ref, f32[256,1,256]{2,1,0:T(1,128)} %reshape.41.bot_ref, bf16[8192,256]{1,0:T(8,128)(2,1)} %all-gather.2.cloned.1.call-done.d_ref), custom_call_target="tpu_custom_call" | custom-call | flops 9663676416 | bytes 8388608 | tf_op jit(solution)/shard_map/pallas_call | solution.py:107
  306.1 53.8 %shard_map.71 = f32[2304,256]{1,0:T(8,128)} custom-call(f32[2304,256]{1,0:T(8,128)} %bitcast.33), custom_call_target="tpu_custom_call" | custom-call | bytes 23592960 | tf_op jit(solution)/shard_map/pallas_call | solution.py:187
  359.9 3.2 copy.57
  (20 shorter events, 0.3 us)
Async XLA Ops:
  7.2 79.1 %reduce-scatter.2.cloned.1.call-start = ((), (), s32[]{:S(2)}) async-start(), calls=%async_computation.1 | async-start | bytes 5242880 | tf_op jit(solution)/shard_map/reduce_scatter | solution.py:226
  9.2 6.1 %collective-permute-start = (bf16[256,256]{1,0:T(8,128)(2,1)S(1)}, bf16[256,256]{1,0:T(8,128)(2,1)S(1)}, u32[]{:S(2)}, u32[]{:S(2)}) collective-permute-start(bf16[256,256]{1,0:T(8,128)(2,1)S(1)} %bitcast.35), channel_id=1, source_target_pairs={{0,1},{1,2},{2,3},{3,4},{4,5},{5,6},{6,7},{8,9},{9,10},{10,11},{11... | collective-permute-start | bytes 393224 | tf_op jit(solution)/shard_map/ppermute | solution.py:209
  13.2 5.7 %collective-permute-start.1 = (bf16[256,256]{1,0:T(8,128)(2,1)S(1)}, bf16[256,256]{1,0:T(8,128)(2,1)S(1)}, u32[]{:S(2)}, u32[]{:S(2)}) collective-permute-start(bf16[256,256]{1,0:T(8,128)(2,1)S(1)} %bitcast.36), channel_id=1, source_target_pairs={{1,0},{2,1},{3,2},{4,3},{5,4},{6,5},{7,6},{9,8},{10,9},{11,10},{12... | collective-permute-start | bytes 393224 | tf_op jit(solution)/shard_map/ppermute | solution.py:209
  38.9 1.2 copy-start.1
  39.0 8.9 %copy-start = (bf16[3,3,256,256]{3,2,1,0:T(8,128)(2,1)S(1)}, bf16[3,3,256,256]{3,2,1,0:T(8,128)(2,1)}, u32[]{:S(2)}) copy-start(bf16[3,3,256,256]{3,2,1,0:T(8,128)(2,1)} %w_ref.3) | copy-start | bytes 3538948
  39.0 211.4 %all-reduce.2.cloned.1.call-start = ((), (), s32[]{:S(2)}) async-start(), calls=%async_computation.3 | async-start | bytes 2359296 | tf_op jit(solution)/shard_map/psum | solution.py:239
  40.8 7.8 %collective-permute-start.6 = (bf16[1,32,256]{2,0,1:T(2,128)(2,1)S(1)}, bf16[1,32,256]{2,0,1:T(2,128)(2,1)S(1)}, u32[]{:S(2)}, u32[]{:S(2)}) collective-permute-start(bf16[1,32,256]{2,0,1:T(2,128)(2,1)S(1)} %get-tuple-element.11), channel_id=1, source_target_pairs={{0,8},{8,16},{16,24},{1,9},{9,17},{17,25},{2,10},{10,18},{18,26},{... | collective-permute-start | bytes 49160 | tf_op jit(solution)/shard_map/ppermute | solution.py:209
  46.0 5.2 %collective-permute-start.7 = (bf16[1,32,256]{2,0,1:T(2,128)(2,1)S(1)}, bf16[1,32,256]{2,0,1:T(2,128)(2,1)S(1)}, u32[]{:S(2)}, u32[]{:S(2)}) collective-permute-start(bf16[1,32,256]{2,0,1:T(2,128)(2,1)S(1)} %get-tuple-element.12), channel_id=1, source_target_pairs={{8,0},{16,8},{24,16},{9,1},{17,9},{25,17},{10,2},{18,10},{26,18},{... | collective-permute-start | bytes 49160 | tf_op jit(solution)/shard_map/ppermute | solution.py:209
  51.9 7.7 %collective-permute-start.8 = (bf16[66,256]{1,0:T(8,128)(2,1)S(1)}, bf16[66,256]{1,0:T(8,128)(2,1)S(1)}, u32[]{:S(2)}, u32[]{:S(2)}) collective-permute-start(bf16[66,256]{1,0:T(8,128)(2,1)S(1)} %get-tuple-element.6), channel_id=1, source_target_pairs={{0,1},{1,2},{2,3},{3,4},{4,5},{5,6},{6,7},{8,9},{9,10},{10,11},{11... | collective-permute-start | bytes 101384 | tf_op jit(solution)/shard_map/ppermute | solution.py:209
  58.3 5.1 %collective-permute-start.9 = (bf16[66,256]{1,0:T(8,128)(2,1)S(1)}, bf16[66,256]{1,0:T(8,128)(2,1)S(1)}, u32[]{:S(2)}, u32[]{:S(2)}) collective-permute-start(bf16[66,256]{1,0:T(8,128)(2,1)S(1)} %get-tuple-element.5), channel_id=1, source_target_pairs={{1,0},{2,1},{3,2},{4,3},{5,4},{6,5},{7,6},{9,8},{10,9},{11,10},{12... | collective-permute-start | bytes 101384 | tf_op jit(solution)/shard_map/ppermute | solution.py:209
  90.0 6.2 %collective-permute-start.3 = (bf16[1,32,256]{2,0,1:T(2,128)(2,1)S(1)}, bf16[1,32,256]{2,0,1:T(2,128)(2,1)S(1)}, u32[]{:S(2)}, u32[]{:S(2)}) collective-permute-start(bf16[1,32,256]{2,0,1:T(2,128)(2,1)S(1)} %copy.37), channel_id=1, source_target_pairs={{8,0},{16,8},{24,16},{9,1},{17,9},{25,17},{10,2},{18,10},{26,18},{... | collective-permute-start | bytes 49160 | tf_op jit(solution)/shard_map/ppermute | solution.py:209
  92.6 4.0 %collective-permute-start.2 = (bf16[1,32,256]{2,0,1:T(2,128)(2,1)S(1)}, bf16[1,32,256]{2,0,1:T(2,128)(2,1)S(1)}, u32[]{:S(2)}, u32[]{:S(2)}) collective-permute-start(bf16[1,32,256]{2,0,1:T(2,128)(2,1)S(1)} %copy.36), channel_id=1, source_target_pairs={{0,8},{8,16},{16,24},{1,9},{9,17},{17,25},{2,10},{10,18},{18,26},{... | collective-permute-start | bytes 49160 | tf_op jit(solution)/shard_map/ppermute | solution.py:209
  97.3 5.6 %collective-permute-start.4 = (bf16[66,256]{1,0:T(8,128)(2,1)S(1)}, bf16[66,256]{1,0:T(8,128)(2,1)S(1)}, u32[]{:S(2)}, u32[]{:S(2)}) collective-permute-start(bf16[66,256]{1,0:T(8,128)(2,1)S(1)} %get-tuple-element.8), channel_id=1, source_target_pairs={{0,1},{1,2},{2,3},{3,4},{4,5},{5,6},{6,7},{8,9},{9,10},{10,11},{11... | collective-permute-start | bytes 101384 | tf_op jit(solution)/shard_map/ppermute | solution.py:209
  101.7 5.4 %collective-permute-start.5 = (bf16[66,256]{1,0:T(8,128)(2,1)S(1)}, bf16[66,256]{1,0:T(8,128)(2,1)S(1)}, u32[]{:S(2)}, u32[]{:S(2)}) collective-permute-start(bf16[66,256]{1,0:T(8,128)(2,1)S(1)} %get-tuple-element.7), channel_id=1, source_target_pairs={{1,0},{2,1},{3,2},{4,3},{5,4},{6,5},{7,6},{9,8},{10,9},{11,10},{12... | collective-permute-start | bytes 101384 | tf_op jit(solution)/shard_map/ppermute | solution.py:209
  117.8 168.9 %all-gather.2.cloned.1.call-start = ((), (), s32[]{:S(2)}) async-start(), calls=%async_computation.2 | async-start | bytes 5242880 | tf_op jit(solution)/shard_map/all_gather | solution.py:233
Sparse Core Ops, SparseCore 0:
  39.1 47.1 reduce-scatter.1
  117.9 132.3 all-reduce.1
  251.9 34.7 all-gather.1

commit v2 on v0

v2 whole, which is shorter than its diff:
```python
import functools

import jax
import jax.numpy as jnp
from jax import lax
from jax.experimental import pallas as pl
from jax.experimental.pallas import tpu as pltpu
from jax.sharding import PartitionSpec as P

MESH = pl.DeviceIdType.MESH
VMEM_LIMIT = 60 * 1024 * 1024
BLOCK = 16
F32 = jnp.float32
BF16 = jnp.bfloat16


def remote(src, dst, send, recv, axis, peer):
    return pltpu.make_async_remote_copy(
        src_ref=src,
        dst_ref=dst,
        send_sem=send,
        recv_sem=recv,
        device_id={axis: peer},
        device_id_type=MESH,
    )


def greet(targets):
    barrier = pltpu.get_barrier_semaphore()
    for axis, peer in targets:
        pl.semaphore_signal(barrier, inc=1, device_id={axis: peer}, device_id_type=MESH)
    pl.semaphore_wait(barrier, len(targets))


def take_edges(shifts, stage):
    rows = shifts.shape[2]

    def one(i, carry):
        c = pl.multiple_of(i * BLOCK, BLOCK)
        x = shifts[1, pl.ds(c, BLOCK)].astype(F32)
        stage[0, pl.ds(c, BLOCK)] = x[:, 0, :].astype(BF16)
        stage[1, pl.ds(c, BLOCK)] = x[:, rows - 1, :].astype(BF16)
        return carry

    lax.fori_loop(0, shifts.shape[1] // BLOCK, one, 0)


def row_copies(stage, halo, send, recv):
    sky = lax.axis_index("sky")
    down = remote(stage.at[0], halo.at[1], send.at[0], recv.at[1], "sky", sky - 1)
    up = remote(stage.at[1], halo.at[0], send.at[1], recv.at[0], "sky", sky + 1)
    return down, up


def send_rows(stage, halo, send, recv):
    sky, count = lax.axis_index("sky"), lax.axis_size("sky")
    down, up = row_copies(stage, halo, send, recv)

    @pl.when(sky > 0)
    def _():
        down.start()

    @pl.when(sky < count - 1)
    def _():
        up.start()

    @pl.when(sky == 0)
    def _():
        halo[0] = jnp.zeros(halo.shape[1:], halo.dtype)

    @pl.when(sky == count - 1)
    def _():
        halo[1] = jnp.zeros(halo.shape[1:], halo.dtype)


def land_rows(stage, halo, send, recv):
    sky, count = lax.axis_index("sky"), lax.axis_size("sky")
    down, up = row_copies(stage, halo, send, recv)

    @pl.when(sky > 0)
    def _():
        down.wait_send()
        up.wait_recv()

    @pl.when(sky < count - 1)
    def _():
        up.wait_send()
        down.wait_recv()


def column_copies(shifts, strip, send, recv):
    freq = lax.axis_index("freq")
    down = remote(shifts.at[1, 1], shifts.at[1, strip + 1], send.at[0], recv.at[1], "freq", freq - 1)
    up = remote(shifts.at[1, strip], shifts.at[1, 0], send.at[1], recv.at[0], "freq", freq + 1)
    return down, up


def send_columns(shifts, strip, send, recv):
    freq, count = lax.axis_index("freq"), lax.axis_size("freq")
    down, up = column_copies(shifts, strip, send, recv)
    line = jnp.zeros(shifts.shape[2:], shifts.dtype)

    @pl.when(freq > 0)
    def _():
        down.start()

    @pl.when(freq < count - 1)
    def _():
        up.start()

    @pl.when(freq == 0)
    def _():
        shifts[1, 0] = line

    @pl.when(freq == count - 1)
    def _():
        shifts[1, strip + 1] = line


def land_columns(shifts, strip, send, recv):
    freq, count = lax.axis_index("freq"), lax.axis_size("freq")
    down, up = column_copies(shifts, strip, send, recv)

    @pl.when(freq > 0)
    def _():
        down.wait_send()
        up.wait_recv()

    @pl.when(freq < count - 1)
    def _():
        up.wait_send()
        down.wait_recv()


def clear_tail(shifts, used):
    shifts[1, used:] = jnp.zeros((shifts.shape[1] - used,) + shifts.shape[2:], shifts.dtype)


def build_shifts(shifts, halo):
    rows, chans = shifts.shape[2:]
    step = BLOCK
    row = lax.broadcasted_iota(jnp.int32, (step, rows, chans), 1)

    def one(i, carry):
        c = pl.multiple_of(i * step, step)
        wide = shifts[1, pl.ds(c, step)].astype(F32)
        top = jnp.broadcast_to(halo[0, pl.ds(c, step)].astype(F32)[:, None, :], wide.shape)
        bot = jnp.broadcast_to(halo[1, pl.ds(c, step)].astype(F32)[:, None, :], wide.shape)
        up = jnp.where(row == 0, top, pltpu.roll(wide, 1, 1))
        down = jnp.where(row == rows - 1, bot, pltpu.roll(wide, rows - 1, 1))
        shifts[0, pl.ds(c, step)] = up.astype(BF16)
        shifts[2, pl.ds(c, step)] = down.astype(BF16)
        return carry

    lax.fori_loop(0, shifts.shape[1] // step, one, 0)


def conv_block(shifts, c, w_ref):
    rows, chans = shifts.shape[2:]
    total = None
    for q in range(3):
        for p in range(3):
            piece = shifts[q, pl.ds(c + p, BLOCK)].reshape(BLOCK * rows, chans)
            term = jnp.dot(piece, w_ref[p, q], preferred_element_type=F32)
            total = term if total is None else total + term
    return total


def add_grad(shifts, c, cols, d_ref, flipped, sums):
    rows, chans = shifts.shape[2:]
    span = cols * rows
    for k in range(span // 256):
        flipped[:, k * 256 : (k + 1) * 256] = d_ref[k * 256 : (k + 1) * 256].T
    for q in range(3):
        for p in range(3):
            piece = shifts[q, pl.ds(c + p, cols)].reshape(span, chans)
            sums[p, q] += jnp.dot(flipped[...], piece, preferred_element_type=F32)


def main_kernel(
    x_hbm, w1_ref, w2_ref, w2b_ref, cot_ref,
    feat_ref, g1_ref, g2_ref,
    xs, cs, hs, xstage, xhalo, cstage, chalo, hstage, hhalo,
    give, got, part, mid, landed, own, back, dall, flipped,
    load_sem, row_send, row_recv, col_send, col_recv,
    give_send, give_recv, mid_send, mid_recv,
    far_send, far_recv, near_send, near_recv, pass_send, pass_recv,
):
    freq, nf = lax.axis_index("freq"), lax.axis_size("freq")
    sky, ns = lax.axis_index("sky"), lax.axis_size("sky")
    ny = nf // 2
    y, core = freq // 2, freq % 2
    partner = y * 2 + 1 - core
    count, rows = x_hbm.shape[:2]
    strip = count // nf
    blocks = strip // BLOCK
    size = BLOCK * rows

    load = pltpu.make_async_copy(x_hbm, xs.at[1, pl.ds(1, count)], load_sem)
    load.start()
    xs[1, 0] = jnp.zeros(xs.shape[2:], BF16)
    clear_tail(xs, count + 1)
    clear_tail(cs, strip + 2)
    clear_tail(hs, strip + 2)
    cs[1, 1 : strip + 1] = cot_ref[...]
    greet(
        [("freq", lax.rem(freq + k, nf)) for k in range(1, nf)]
        + [("sky", lax.rem(sky + 1, ns)), ("sky", lax.rem(sky + ns - 1, ns))]
    )
    send_columns(cs, strip, col_send.at[0], col_recv.at[0])
    load.wait()
    take_edges(xs, xstage)
    send_rows(xstage, xhalo, row_send.at[0], row_recv.at[0])
    land_columns(cs, strip, col_send.at[0], col_recv.at[0])
    take_edges(cs, cstage)
    send_rows(cstage, chalo, row_send.at[1], row_recv.at[1])
    land_rows(xstage, xhalo, row_send.at[0], row_recv.at[0])
    build_shifts(xs, xhalo)

    def give_copy(t):
        return remote(
            give.at[t], got.at[t], give_send.at[t], give_recv.at[t], "freq", partner
        )

    def mid_copy(t):
        peer = lax.rem(y + 1 + t // blocks, ny) * 2 + core
        return remote(mid.at[t], landed.at[t], mid_send.at[t], mid_recv.at[t], "freq", peer)

    away = (ny - 1) * blocks
    steps = ny * blocks

    def one(t, carry):
        @pl.when(t < steps)
        def _():
            dest = lax.rem(y + 1 + t // blocks, ny) * 2
            sub = lax.rem(t, blocks) * BLOCK
            give[t] = conv_block(xs, (dest + 1 - core) * strip + sub, w1_ref).astype(BF16)
            give_copy(t).start()
            part[lax.rem(t, 2)] = conv_block(xs, (dest + core) * strip + sub, w1_ref)

        @pl.when(t > 0)
        def _():
            before = t - 1
            give_copy(before).wait_recv()
            total = part[lax.rem(before, 2)] + got[before].astype(F32)

            @pl.when(before < away)
            def _():
                mid[before] = total.astype(BF16)
                mid_copy(before).start()

            @pl.when(before >= away)
            def _():
                own[before - away] = total

        return carry

    lax.fori_loop(0, steps + 1, one, 0)

    land_rows(cstage, chalo, row_send.at[1], row_recv.at[1])
    build_shifts(cs, chalo)

    def one_back(i, carry):
        back[i] = conv_block(cs, i * BLOCK, w2b_ref)
        return carry

    lax.fori_loop(0, blocks, one_back, 0)

    def one_pre(i, carry):
        pre = own[i]
        for dy in range(ny - 1):
            mid_copy(dy * blocks + i).wait_recv()
            pre = pre + landed[dy * blocks + i].astype(F32)
        sigma = jax.nn.sigmoid(pre)
        hs[1, pl.ds(1 + i * BLOCK, BLOCK)] = (pre * sigma).astype(BF16).reshape(BLOCK, rows, -1)
        delta = back[i] * sigma * (1.0 + pre * (1.0 - sigma))
        dall[freq, pl.ds(pl.multiple_of(i * size, size), size)] = delta.astype(BF16)
        return carry

    lax.fori_loop(0, blocks, one_pre, 0)

    send_columns(hs, strip, col_send.at[1], col_recv.at[1])

    def far_copy(dy):
        peer = lax.rem(y + dy, ny) * 2 + core
        return remote(
            dall.at[freq], dall.at[freq], far_send.at[dy - 1], far_recv.at[dy - 1], "freq", peer
        )

    def pass_copy(dy):
        owner = lax.rem(y + ny - dy, ny) * 2 + core
        return remote(
            dall.at[owner], dall.at[owner], pass_send.at[dy - 1], pass_recv.at[dy - 1],
            "freq", partner,
        )

    near = remote(dall.at[freq], dall.at[freq], near_send, near_recv, "freq", partner)
    for dy in range(1, ny):
        far_copy(dy).start()
    near.start()
    land_columns(hs, strip, col_send.at[1], col_recv.at[1])
    take_edges(hs, hstage)
    send_rows(hstage, hhalo, row_send.at[2], row_recv.at[2])

    g1_ref[...] = jnp.zeros_like(g1_ref)
    g2_ref[...] = jnp.zeros_like(g2_ref)
    add_grad(xs, freq * strip, strip, dall.at[freq], flipped, g1_ref)
    land_rows(hstage, hhalo, row_send.at[2], row_recv.at[2])
    build_shifts(hs, hhalo)

    def one_feature(i, carry):
        value = conv_block(hs, i * BLOCK, w2_ref)
        feat_ref[pl.ds(pl.multiple_of(i * size, size), size)] = value.astype(feat_ref.dtype)
        return carry

    lax.fori_loop(0, blocks, one_feature, 0)
    near.wait_recv()
    add_grad(xs, partner * strip, strip, dall.at[partner], flipped, g1_ref)
    add_grad(hs, 0, strip, cot_ref.reshape(strip * rows, -1), flipped, g2_ref)
    for dy in range(1, ny):
        far_copy(dy).wait_recv()
        pass_copy(dy).start()
        owner = lax.rem(y + ny - dy, ny) * 2
        add_grad(xs, (owner + core) * strip, strip, dall.at[owner + core], flipped, g1_ref)
    for dy in range(1, ny):
        pass_copy(dy).wait_recv()
        owner = lax.rem(y + ny - dy, ny) * 2
        add_grad(xs, (owner + 1 - core) * strip, strip, dall.at[owner + 1 - core], flipped, g1_ref)

    def drain(t, carry):
        give_copy(t).wait_send()

        @pl.when(t < away)
        def _():
            mid_copy(t).wait_send()

        return carry

    lax.fori_loop(0, steps, drain, 0)
    near.wait_send()
    for dy in range(1, ny):
        far_copy(dy).wait_send()
        pass_copy(dy).wait_send()


def main_call(x, w1, w2, w2b, cot):
    nf = lax.axis_size("freq")
    ny = nf // 2
    count, rows, chans = x.shape
    strip, _, outs = cot.shape
    hid = w1.shape[3]
    blocks = strip // BLOCK
    size = BLOCK * rows
    steps, away = ny * blocks, (ny - 1) * blocks
    wide, thin = count + BLOCK, strip + BLOCK
    vmem = pl.BlockSpec(memory_space=pltpu.VMEM)
    dma = pltpu.SemaphoreType.DMA
    return pl.pallas_call(
        main_kernel,
        out_shape=(
            jax.ShapeDtypeStruct((strip * rows, outs), BF16),
            jax.ShapeDtypeStruct((3, 3, hid, chans), F32),
            jax.ShapeDtypeStruct((3, 3, outs, hid), F32),
        ),
        in_specs=[pl.BlockSpec(memory_space=pl.ANY)] + [vmem] * 4,
        out_specs=(vmem,) * 3,
        scratch_shapes=[
            pltpu.VMEM((3, wide, rows, chans), BF16),
            pltpu.VMEM((3, thin, rows, outs), BF16),
            pltpu.VMEM((3, thin, rows, hid), BF16),
            pltpu.VMEM((2, wide, chans), BF16),
            pltpu.VMEM((2, wide, chans), BF16),
            pltpu.VMEM((2, thin, outs), BF16),
            pltpu.VMEM((2, thin, outs), BF16),
            pltpu.VMEM((2, thin, hid), BF16),
            pltpu.VMEM((2, thin, hid), BF16),
            pltpu.VMEM((steps, size, hid), BF16),
            pltpu.VMEM((steps, size, hid), BF16),
            pltpu.VMEM((2, size, hid), F32),
            pltpu.VMEM((away, size, hid), BF16),
            pltpu.VMEM((away, size, hid), BF16),
            pltpu.VMEM((blocks, size, hid), F32),
            pltpu.VMEM((blocks, size, hid), F32),
            pltpu.VMEM((nf, strip * rows, hid), BF16),
            pltpu.VMEM((hid, strip * rows), BF16),
            dma,
            dma((3, 2)), dma((3, 2)), dma((2, 2)), dma((2, 2)),
            dma((steps,)), dma((steps,)), dma((away,)), dma((away,)),
            dma((ny - 1,)), dma((ny - 1,)), dma, dma, dma((ny - 1,)), dma((ny - 1,)),
        ],
        compiler_params=pltpu.CompilerParams(
            collective_id=1, has_side_effects=True, vmem_limit_bytes=VMEM_LIMIT
        ),
        cost_estimate=pl.CostEstimate(
            flops=36 * count * rows * chans * hid, bytes_accessed=4 * x.size, transcendentals=0
        ),
    )(x, w1, w2, w2b, cot)


def sum_kernel(
    g1_ref, g2_ref, o1_ref, o2_ref,
    mine1, landed1, full1, mine2, landed2, share, landed3, full3, full4, full2,
    s1, r1, s2, r2, s3, r3, s4, r4, s5, r5, s6, r6,
):
    freq, nf = lax.axis_index("freq"), lax.axis_size("freq")
    sky, ns = lax.axis_index("sky"), lax.axis_size("sky")
    chunk1 = g1_ref.shape[0] // ns
    chunk2 = g2_ref.shape[0] // nf
    chunk3 = share.shape[0] // ns

    def rows_of(i, chunk):
        return pl.ds(pl.multiple_of(i * chunk, 16), chunk)

    def scatter(axis, me, n, src, dst, chunk, send, recv):
        out = []
        for k in range(1, n):
            peer = lax.rem(me + k, n)
            out.append(
                remote(src.at[rows_of(peer, chunk)], dst.at[k - 1], send.at[k - 1],
                       recv.at[k - 1], axis, peer)
            )
        return out

    def gather(axis, me, n, full, chunk, send, recv):
        here = full.at[rows_of(me, chunk)]
        return [
            remote(here, here, send.at[k - 1], recv.at[k - 1], axis, lax.rem(me + k, n))
            for k in range(1, n)
        ]

    def start(copies):
        for copy in copies:
            copy.start()

    def collect(copies, landed, total):
        for k, copy in enumerate(copies):
            copy.wait_recv()
            total = total + landed[k].astype(F32)
        return total

    mine1[...] = g1_ref[...].astype(BF16)
    mine2[...] = g2_ref[...].astype(BF16)
    share[chunk2:] = jnp.zeros((share.shape[0] - chunk2, share.shape[1]), F32)
    greet(
        [("freq", lax.rem(freq + k, nf)) for k in range(1, nf)]
        + [("sky", lax.rem(sky + k, ns)) for k in range(1, ns)]
    )
    a2 = scatter("freq", freq, nf, mine2, landed2, chunk2, s2, r2)
    start(a2)
    a1 = scatter("sky", sky, ns, mine1, landed1, chunk1, s1, r1)
    start(a1)
    share[:chunk2] = collect(a2, landed2, g2_ref[rows_of(freq, chunk2)])
    full3[...] = share[...].astype(BF16)
    a3 = scatter("sky", sky, ns, full3, landed3, chunk3, s3, r3)
    start(a3)
    full1[rows_of(sky, chunk1)] = collect(a1, landed1, g1_ref[rows_of(sky, chunk1)]).astype(BF16)
    b1 = gather("sky", sky, ns, full1, chunk1, s4, r4)
    start(b1)
    total3 = collect(a3, landed3, share[rows_of(sky, chunk3)])
    full4[rows_of(sky, chunk3)] = total3.astype(BF16)
    b3 = gather("sky", sky, ns, full4, chunk3, s5, r5)
    start(b3)
    for copy in b3:
        copy.wait_recv()
    full2[rows_of(freq, chunk2)] = full4[:chunk2]
    b2 = gather("freq", freq, nf, full2, chunk2, s6, r6)
    start(b2)
    for copy in b1:
        copy.wait_recv()
    o1_ref[...] = full1[...].astype(F32)
    for copy in b2:
        copy.wait_recv()
    o2_ref[...] = full2[...].astype(F32)
    for copy in a1 + a2 + a3 + b1 + b2 + b3:
        copy.wait_send()


def sum_call(g1, g2):
    nf, ns = lax.axis_size("freq"), lax.axis_size("sky")
    rows1, cols1 = g1.shape
    rows2, cols2 = g2.shape
    chunk1, chunk2 = rows1 // ns, rows2 // nf
    chunk3 = -(-chunk2 // (16 * ns)) * 16
    vmem = pl.BlockSpec(memory_space=pltpu.VMEM)
    dma = pltpu.SemaphoreType.DMA
    along = [dma((ns - 1,))] * 2
    across = [dma((nf - 1,))] * 2
    return pl.pallas_call(
        sum_kernel,
        out_shape=(
            jax.ShapeDtypeStruct((rows1, cols1), F32),
            jax.ShapeDtypeStruct((rows2, cols2), F32),
        ),
        in_specs=[vmem] * 2,
        out_specs=(vmem,) * 2,
        scratch_shapes=[
            pltpu.VMEM((rows1, cols1), BF16),
            pltpu.VMEM((ns - 1, chunk1, cols1), BF16),
            pltpu.VMEM((rows1, cols1), BF16),
            pltpu.VMEM((rows2, cols2), BF16),
            pltpu.VMEM((nf - 1, chunk2, cols2), BF16),
            pltpu.VMEM((ns * chunk3, cols2), F32),
            pltpu.VMEM((ns - 1, chunk3, cols2), BF16),
            pltpu.VMEM((ns * chunk3, cols2), BF16),
            pltpu.VMEM((ns * chunk3, cols2), BF16),
            pltpu.VMEM((rows2, cols2), BF16),
        ]
        + along + across + along + along + along + across,
        compiler_params=pltpu.CompilerParams(
            collective_id=0, has_side_effects=True, vmem_limit_bytes=VMEM_LIMIT
        ),
        cost_estimate=pl.CostEstimate(flops=0, bytes_accessed=40 * g1.size, transcendentals=0),
    )(g1, g2)


def body(sky_cube, weight_first, weight_second, cotangent):
    strip, rows, _ = cotangent.shape
    weight_back = jnp.transpose(weight_second[::-1, ::-1], (0, 1, 3, 2))
    features, first, second = main_call(
        sky_cube, weight_first, weight_second, weight_back, cotangent
    )
    sum_first, sum_second = sum_call(
        first.reshape(-1, first.shape[3]), second.reshape(-1, second.shape[3])
    )
    grad_first = jnp.transpose(sum_first.reshape(first.shape), (0, 1, 3, 2))
    grad_second = jnp.transpose(sum_second.reshape(second.shape), (0, 1, 3, 2))
    return (features.reshape(strip, rows, -1), grad_first, grad_second)


def solution(mesh):
    return jax.shard_map(
        body,
        mesh=mesh,
        in_specs=(P(None, "sky", "freq"), P(None, None, "freq", None), P(), P("freq", "sky", None)),
        out_specs=(P("freq", "sky", None), P(None, None, "freq", None), P()),
        check_vma=False,
    )
```

time: 503 us -> 178 us (0.35); the launches traced: 493 us -> 178 us
  waiting for transfers between devices: 232 us -> 0 us
  Pallas kernels: 0 us -> 169 us
  local copies, waits for them, and re-layouts: 125 us -> 8.79 us
  matrix products: 59.3 us -> 0 us
  other arithmetic: 33.4 us -> 0 us
  starting transfers between devices: 28.6 us -> 0 us
  between operations: 14.9 us -> 0.66 us
    psum x2 -> x0, waiting for transfers between devices: 203 us -> none  [the longest x1 137 us: body(): grad_second = lax.psum(second_part, ('freq', 'sky'))]
    pallas_call x0 -> x2, Pallas kernels: none -> 169 us  [the longest x1 89.4 us: sum_call(): pl.pallas_call(sum_kernel, out_shape=(jax.ShapeDtypeStruct((rows1, cols1)...]
    slice x22 -> x0, local copies, waits for them, and re-layouts: 96.3 us -> none  [the longest x18 95.1 us: conv_taps(): padded[tap_col:tap_col + col_count, tap_row:tap_row + row_count]]
    dot_general x45 -> x0, matrix products: 59.3 us -> none  [the longest x18 33.5 us: kernel_grad(): lax.dot_general(piece, flat, (((0,), (0,)), ((), ())), preferred_element_...]
    ppermute x10 -> x0, starting transfers between devices: 28.5 us -> none  [the longest x5 20 us: with_halo(): before = lax.ppermute(last, axis, up)]
    reduce_scatter x1 -> x0, waiting for transfers between devices: 20.6 us -> none  [body(): lax.psum_scatter(conv_taps(slab, weight_first, strip * lax.axis_size('fre...]
    unnamed x55 -> x6, local copies, waits for them, and re-layouts: 21.9 us -> 2.55 us
    concatenate x6 -> x0, other arithmetic: 14.1 us -> none  [with_halo(): x = jnp.concatenate([before, x, after], axis=dim)]
  transfers between devices with their start and end apart: 14 -> 0, of which waited for: 7 -> 0; matrix products, arithmetic and copies ran while one was open for 11% -> 0% of each run, Pallas kernels for 0% -> 0%
where the time goes in v2:
time: 178 us
  Pallas kernels  169 us (95%)
  local copies, waits for them, and re-layouts  8.79 us (5%)
    pallas_call x1, Pallas kernels, sum_call(): pl.pallas_call(sum_kernel, out_shape=(jax.ShapeDtypeStruct((rows1, cols1)...  89.4 us
    pallas_call x1, Pallas kernels, main_call(): pl.pallas_call(main_kernel, out_shape=(jax.ShapeDtypeStruct((strip * rows...  79.2 us

profile of v2, /device:TPU:1, one launch (start us, length us, event | category | flops | bytes accessed | tf_op | source)
XLA Modules:
  0.0 178.1 jit_solution(15078814679990760063)
XLA Ops:
  0.6 1.6 copy.7
  2.2 1.1 reverse_bitcast_fusion.w2b_ref
  3.3 79.2 %shard_map.67 = (bf16[2048,256]{1,0:T(8,128)(2,1)}, f32[3,3,256,256]{3,2,1,0:T(8,128)}, f32[3,3,256,256]{3,2,1,0:T(8,128)}) custom-call(bf16[256,32,256]{2,1,0:T(8,128)(2,1)} %x_hbm.1, bf16[3,3,256,256]{3,2,1,0:T(8,128)(2,1)} %w1_ref.1, bf16[3,3,256,256]{3,2,1,0:T(8,128)(2,1)} %w2_ref.1, bf16[3,3,256,256]{3,2,1,0:T(8,128)(2,1)} %reverse_bitcast_fusion.w2b_ref, ...), custom_call_target="tpu_custom_call" | custom-call | flops 19327352832 | bytes 8388608 | tf_op jit(solution)/shard_map/pallas_call | solution.py:358
  82.6 89.4 %shard_map.68 = (f32[2304,256]{1,0:T(8,128)}, f32[2304,256]{1,0:T(8,128)}) custom-call(f32[2304,256]{1,0:T(8,128)} %bitcast.11, f32[2304,256]{1,0:T(8,128)} %bitcast.12), custom_call_target="tpu_custom_call" | custom-call | bytes 23592960 | tf_op jit(solution)/shard_map/pallas_call | solution.py:488
  171.9 0.0 copy-start
  172.0 3.2 %copy.8 = f32[3,3,256,256]{2,3,1,0:T(8,128)} copy(f32[3,3,256,256]{3,2,1,0:T(8,128)} %bitcast.14) | data formatting | bytes 4718592 | tf_op jit(solution)/shard_map/reshape | solution.py:525
  175.2 0.0 copy-done
  175.2 0.0 copy-start.1
  175.2 1.9 %copy.9 = f32[3,3,256,256]{2,3,1,0:T(8,128)} copy(f32[3,3,256,256]{3,2,1,0:T(8,128)S(1)} %bitcast.13) | data formatting | bytes 4718592 | tf_op jit(solution)/shard_map/reshape | solution.py:526
  177.1 0.0 copy-done.1
  177.1 1.0 copy.11
Async XLA Ops:
  171.9 3.2 %copy-start = (f32[2304,256]{1,0:T(8,128)S(1)}, f32[2304,256]{1,0:T(8,128)}, u32[]{:S(2)}) copy-start(f32[2304,256]{1,0:T(8,128)} %get-tuple-element.12) | copy-start | bytes 7077892
  175.2 1.9 %copy-start.1 = (bf16[2048,256]{1,0:T(8,128)(2,1)S(1)}, bf16[2048,256]{1,0:T(8,128)(2,1)}, u32[]{:S(2)}) copy-start(bf16[2048,256]{1,0:T(8,128)(2,1)} %get-tuple-element.8) | copy-start | bytes 3145732

commit v3 on v2

--- a/solution.py
+++ b/solution.py
@@ -157,13 +157,16 @@
 
 def conv_block(shifts, c, w_ref):
     rows, chans = shifts.shape[2:]
-    total = None
-    for q in range(3):
-        for p in range(3):
-            piece = shifts[q, pl.ds(c + p, BLOCK)].reshape(BLOCK * rows, chans)
-            term = jnp.dot(piece, w_ref[p, q], preferred_element_type=F32)
-            total = term if total is None else total + term
-    return total
+    pieces = [
+        shifts[q, pl.ds(c + p, BLOCK)].reshape(BLOCK * rows, chans)
+        for p in range(3)
+        for q in range(3)
+    ]
+    return jnp.dot(
+        jnp.concatenate(pieces, axis=1),
+        w_ref[...].reshape(9 * chans, -1),
+        preferred_element_type=F32,
+    )
 
 
 def add_grad(shifts, c, cols, d_ref, flipped, sums):
@@ -397,96 +400,201 @@
     )(x, w1, w2, w2b, cot)
 
 
-def sum_kernel(
-    g1_ref, g2_ref, o1_ref, o2_ref,
-    mine1, landed1, full1, mine2, landed2, share, landed3, full3, full4, full2,
-    s1, r1, s2, r2, s3, r3, s4, r4, s5, r5, s6, r6,
-):
+def sum_kernel(pieces, nx, g1_ref, g2_ref, o1_ref, o2_ref, *refs):
+    refs = list(refs)
     freq, nf = lax.axis_index("freq"), lax.axis_size("freq")
     sky, ns = lax.axis_index("sky"), lax.axis_size("sky")
-    chunk1 = g1_ref.shape[0] // ns
-    chunk2 = g2_ref.shape[0] // nf
-    chunk3 = share.shape[0] // ns
-
-    def rows_of(i, chunk):
-        return pl.ds(pl.multiple_of(i * chunk, 16), chunk)
-
-    def scatter(axis, me, n, src, dst, chunk, send, recv):
-        out = []
-        for k in range(1, n):
-            peer = lax.rem(me + k, n)
-            out.append(
-                remote(src.at[rows_of(peer, chunk)], dst.at[k - 1], send.at[k - 1],
-                       recv.at[k - 1], axis, peer)
-            )
-        return out
-
-    def gather(axis, me, n, full, chunk, send, recv):
-        here = full.at[rows_of(me, chunk)]
-        return [
-            remote(here, here, send.at[k - 1], recv.at[k - 1], axis, lax.rem(me + k, n))
-            for k in range(1, n)
-        ]
+    ny, nz = nf // 2, ns // nx
+    y, core = freq // 2, freq % 2
+    z, x = sky // nx, sky % nx
+    partner = y * 2 + 1 - core
+    half = g2_ref.shape[0] // 2
+    chunk = half // ny
+    side, side_in, mine2, side_y, landed2, joined, full2 = refs[:7]
+    core_sems, y_sems, x_sems, z_sems = refs[7:11]
+    rest = refs[11:]
+    sets = [rest[6 * i : 6 * i + 6] for i in range(len(pieces))]
+
+    def rows_of(i, size):
+        return pl.ds(pl.multiple_of(i * size, 16), size)
 
     def start(copies):
         for copy in copies:
             copy.start()
-
-    def collect(copies, landed, total):
-        for k, copy in enumerate(copies):
+        return copies
+
+    def land(copies):
+        for copy in copies:
             copy.wait_recv()
-            total = total + landed[k].astype(F32)
-        return total
-
-    mine1[...] = g1_ref[...].astype(BF16)
-    mine2[...] = g2_ref[...].astype(BF16)
-    share[chunk2:] = jnp.zeros((share.shape[0] - chunk2, share.shape[1]), F32)
+
+    def x_peer(k):
+        return z * nx + lax.rem(x + k, nx)
+
+    def z_peer(k):
+        return lax.rem(z + k, nz) * nx + x
+
+    def y_peer(k):
+        return lax.rem(y + k, ny)
+
     greet(
-        [("freq", lax.rem(freq + k, nf)) for k in range(1, nf)]
-        + [("sky", lax.rem(sky + k, ns)) for k in range(1, ns)]
+        [("freq", partner)]
+        + [("freq", y_peer(k) * 2 + core) for k in range(1, ny)]
+        + [("sky", x_peer(k)) for k in range(1, nx)]
+        + [("sky", z_peer(k)) for k in range(1, nz)]
     )
-    a2 = scatter("freq", freq, nf, mine2, landed2, chunk2, s2, r2)
-    start(a2)
-    a1 = scatter("sky", sky, ns, mine1, landed1, chunk1, s1, r1)
-    start(a1)
-    share[:chunk2] = collect(a2, landed2, g2_ref[rows_of(freq, chunk2)])
-    full3[...] = share[...].astype(BF16)
-    a3 = scatter("sky", sky, ns, full3, landed3, chunk3, s3, r3)
-    start(a3)
-    full1[rows_of(sky, chunk1)] = collect(a1, landed1, g1_ref[rows_of(sky, chunk1)]).astype(BF16)
-    b1 = gather("sky", sky, ns, full1, chunk1, s4, r4)
-    start(b1)
-    total3 = collect(a3, landed3, share[rows_of(sky, chunk3)])
-    full4[rows_of(sky, chunk3)] = total3.astype(BF16)
-    b3 = gather("sky", sky, ns, full4, chunk3, s5, r5)
-    start(b3)
-    for copy in b3:
-        copy.wait_recv()
-    full2[rows_of(freq, chunk2)] = full4[:chunk2]
-    b2 = gather("freq", freq, nf, full2, chunk2, s6, r6)
-    start(b2)
-    for copy in b1:
-        copy.wait_recv()
-    o1_ref[...] = full1[...].astype(F32)
-    for copy in b2:
-        copy.wait_recv()
-    o2_ref[...] = full2[...].astype(F32)
-    for copy in a1 + a2 + a3 + b1 + b2 + b3:
+    done = []
+    side[...] = g2_ref[rows_of(1 - core, half)].astype(BF16)
+    core_out = remote(side, side_in, core_sems.at[0, 0], core_sems.at[0, 1], "freq", partner)
+    done += start([core_out])
+
+    def x_scatter(i):
+        src, land_x = sets[i][0], sets[i][1]
+        size = pieces[i][1] // nx
+        return start([
+            remote(src.at[rows_of(lax.rem(x + k, nx), size)], land_x.at[k - 1],
+                   x_sems.at[0, i, k - 1], x_sems.at[1, i, k - 1], "sky", x_peer(k))
+            for k in range(1, nx)
+        ])
+
+    def z_scatter(i):
+        mid, land_z = sets[i][3], sets[i][4]
+        size = pieces[i][1] // ns
+        return start([
+            remote(mid.at[rows_of(lax.rem(z + k, nz), size)], land_z.at[k - 1],
+                   z_sems.at[0, i, k - 1], z_sems.at[1, i, k - 1], "sky", z_peer(k))
+            for k in range(1, nz)
+        ])
+
+    def z_gather(i):
+        size = pieces[i][1] // ns
+        here = sets[i][5].at[rows_of(x * nz + z, size)]
+        return start([
+            remote(here, here, z_sems.at[2, i, k - 1], z_sems.at[3, i, k - 1], "sky", z_peer(k))
+            for k in range(1, nz)
+        ])
+
+    def x_gather(i):
+        size = pieces[i][1] // nx
+        here = sets[i][5].at[rows_of(x, size)]
+        return start([
+            remote(here, here, x_sems.at[2, i, k - 1], x_sems.at[3, i, k - 1], "sky", x_peer(k))
+            for k in range(1, nx)
+        ])
+
+    count = len(pieces)
+    flights = {}
+    for i in range(count - 1):
+        first, size = pieces[i]
+        sets[i][0][...] = g1_ref[first : first + size].astype(BF16)
+        flights[i] = x_scatter(i)
+
+    core_out.wait_recv()
+    mine2[...] = g2_ref[rows_of(core, half)] + side_in[...].astype(F32)
+    side_y[...] = mine2[...].astype(BF16)
+    y_out = start([
+        remote(side_y.at[rows_of(y_peer(k), chunk)],
+               landed2.at[k - 1], y_sems.at[0, k - 1], y_sems.at[1, k - 1],
+               "freq", y_peer(k) * 2 + core)
+        for k in range(1, ny)
+    ])
+
+    def x_sum(i, own):
+        size = pieces[i][1] // nx
+        land(flights[i])
+        done.extend(flights[i])
+        total = own
+        for k in range(nx - 1):
+            total = total + sets[i][1][k].astype(F32)
+        sets[i][2][...] = total
+        sets[i][3][...] = total.astype(BF16)
+        flights[i] = z_scatter(i)
+
+    def x_sum_first(i):
+        first, rows = pieces[i]
+        size = rows // nx
+        x_sum(i, g1_ref[pl.ds(pl.multiple_of(first + x * size, 16), size)])
+
+    x_sum_first(0)
+    land(y_out)
+    total = mine2[rows_of(y, chunk)]
+    for k in range(ny - 1):
+        total = total + landed2[k].astype(F32)
+    last = count - 1
+    joined[:chunk] = total
+    if joined.shape[0] > chunk:
+        joined[chunk:] = jnp.zeros((joined.shape[0] - chunk, joined.shape[1]), F32)
+    sets[last][0][...] = joined[...].astype(BF16)
+    flights[last] = x_scatter(last)
+    for i in range(1, count - 1):
+        x_sum_first(i)
+    x_sum(last, joined[rows_of(x, pieces[last][1] // nx)])
+
+    order = [0, last] + list(range(1, count - 1))
+    for i in order:
+        size = pieces[i][1] // ns
+        land(flights[i])
+        done.extend(flights[i])
+        total = sets[i][2][rows_of(z, size)]
+        for k in range(nz - 1):
+            total = total + sets[i][4][k].astype(F32)
+        sets[i][5][rows_of(x * nz + z, size)] = total.astype(BF16)
+        flights[i] = z_gather(i)
+    for i in order:
+        land(flights[i])
+        done.extend(flights[i])
+        flights[i] = x_gather(i)
+    land(flights[last])
+    done.extend(flights[last])
+    done.extend(y_out)
+    here = full2.at[pl.ds(pl.multiple_of(core * half + y * chunk, 16), chunk)]
+    here[...] = sets[last][5][:chunk]
+    y_back = start([
+        remote(here, here, y_sems.at[2, k - 1], y_sems.at[3, k - 1], "freq", y_peer(k) * 2 + core)
+        for k in range(1, ny)
+    ])
+    done.extend(y_back)
+    for i in range(count - 1):
+        first, size = pieces[i]
+        land(flights[i])
+        done.extend(flights[i])
+        o1_ref[first : first + size] = sets[i][5][...].astype(F32)
+    land(y_back)
+    ours = full2.at[rows_of(core, half)]
+    core_back = remote(ours, ours, core_sems.at[1, 0], core_sems.at[1, 1], "freq", partner)
+    done += start([core_back])
+    o2_ref[rows_of(core, half)] = ours[...].astype(F32)
+    core_back.wait_recv()
+    o2_ref[rows_of(1 - core, half)] = full2[rows_of(1 - core, half)].astype(F32)
+    for copy in done:
         copy.wait_send()
 
 
 def sum_call(g1, g2):
     nf, ns = lax.axis_size("freq"), lax.axis_size("sky")
+    ny = nf // 2
+    nz = 4 if ns % 4 == 0 else 1
+    nx = ns // nz
     rows1, cols1 = g1.shape
     rows2, cols2 = g2.shape
-    chunk1, chunk2 = rows1 // ns, rows2 // nf
-    chunk3 = -(-chunk2 // (16 * ns)) * 16
+    half, chunk = rows2 // 2, rows2 // nf
+    last = -(-chunk // (16 * ns)) * 16 * ns
+    cut = rows1 // 3
+    pieces = [(i * cut, cut) for i in range(3)] + [(0, last)]
     vmem = pl.BlockSpec(memory_space=pltpu.VMEM)
     dma = pltpu.SemaphoreType.DMA
-    along = [dma((ns - 1,))] * 2
-    across = [dma((nf - 1,))] * 2
+    buffers = []
+    for i, (_, size) in enumerate(pieces):
+        cols = cols1 if i < 3 else cols2
+        buffers += [
+            pltpu.VMEM((size, cols), BF16),
+            pltpu.VMEM((nx - 1, size // nx, cols), BF16),
+            pltpu.VMEM((size // nx, cols), F32),
+            pltpu.VMEM((size // nx, cols), BF16),
+            pltpu.VMEM((nz - 1, size // ns, cols), BF16),
+            pltpu.VMEM((size, cols), BF16),
+        ]
     return pl.pallas_call(
-        sum_kernel,
+        functools.partial(sum_kernel, pieces, nx),
         out_shape=(
             jax.ShapeDtypeStruct((rows1, cols1), F32),
             jax.ShapeDtypeStruct((rows2, cols2), F32),
@@ -494,18 +602,19 @@
         in_specs=[vmem] * 2,
         out_specs=(vmem,) * 2,
         scratch_shapes=[
-            pltpu.VMEM((rows1, cols1), BF16),
-            pltpu.VMEM((ns - 1, chunk1, cols1), BF16),
-            pltpu.VMEM((rows1, cols1), BF16),
+            pltpu.VMEM((half, cols2), BF16),
+            pltpu.VMEM((half, cols2), BF16),
+            pltpu.VMEM((half, cols2), F32),
+            pltpu.VMEM((half, cols2), BF16),
+            pltpu.VMEM((ny - 1, chunk, cols2), BF16),
+            pltpu.VMEM((last, cols2), F32),
             pltpu.VMEM((rows2, cols2), BF16),
-            pltpu.VMEM((nf - 1, chunk2, cols2), BF16),
-            pltpu.VMEM((ns * chunk3, cols2), F32),
-            pltpu.VMEM((ns - 1, chunk3, cols2), BF16),
-            pltpu.VMEM((ns * chunk3, cols2), BF16),
-            pltpu.VMEM((ns * chunk3, cols2), BF16),
-            pltpu.VMEM((rows2, cols2), BF16),
+            dma((2, 2)),
+            dma((4, ny - 1)),
+            dma((4, 4, nx - 1)),
+            dma((4, 4, nz - 1)),
         ]
-        + along + across + along + along + along + across,
+        + buffers,
         compiler_params=pltpu.CompilerParams(
             collective_id=0, has_side_effects=True, vmem_limit_bytes=VMEM_LIMIT
         ),

time: 178 us -> 149 us (0.84)
  Pallas kernels: 169 us -> 139 us
    pallas_call x1, Pallas kernels: 89.4 us -> 60.1 us  [sum_call(): pl.pallas_call(functools.partial(sum_kernel, pieces, nx), out_shape=(jax....]
where the time goes in v3:
time: 149 us
  Pallas kernels  139 us (93%)
  local copies, waits for them, and re-layouts  8.79 us (6%)
    pallas_call x1, Pallas kernels, main_call(): pl.pallas_call(main_kernel, out_shape=(jax.ShapeDtypeStruct((strip * rows...  79.2 us
    pallas_call x1, Pallas kernels, sum_call(): pl.pallas_call(functools.partial(sum_kernel, pieces, nx), out_shape=(jax....  60.1 us
    reshape x1, local copies, waits for them, and re-layouts, body(): grad_first = jnp.transpose(sum_first.reshape(first.shape), (0, 1, 3, 2))  3.2 us

profile of v3, /device:TPU:1, one launch (start us, length us, event | category | flops | bytes accessed | tf_op | source)
XLA Modules:
  0.0 148.8 jit_solution(612422351445363703)
XLA Ops:
  0.6 1.6 %copy.7 = bf16[3,3,256,256]{2,3,1,0:T(8,128)(2,1)S(1)} copy(bf16[3,3,256,256]{3,2,1,0:T(8,128)(2,1)} %w2_ref.1) | data formatting | bytes 2359296 | tf_op args[2]
  2.2 1.1 reverse_bitcast_fusion.w2b_ref
  3.3 79.2 %shard_map.67 = (bf16[2048,256]{1,0:T(8,128)(2,1)}, f32[3,3,256,256]{3,2,1,0:T(8,128)}, f32[3,3,256,256]{3,2,1,0:T(8,128)}) custom-call(bf16[256,32,256]{2,1,0:T(8,128)(2,1)} %x_hbm.1, bf16[3,3,256,256]{3,2,1,0:T(8,128)(2,1)} %w1_ref.1, bf16[3,3,256,256]{3,2,1,0:T(8,128)(2,1)} %w2_ref.1, bf16[3,3,256,256]{3,2,1,0:T(8,128)(2,1)} %reverse_bitcast_fusion.w2b_ref, ...), custom_call_target="tpu_custom_call" | custom-call | flops 19327352832 | bytes 8388608 | tf_op jit(solution)/shard_map/pallas_call | solution.py:361
  82.6 60.1 %shard_map.68 = (f32[2304,256]{1,0:T(8,128)}, f32[2304,256]{1,0:T(8,128)}) custom-call(f32[2304,256]{1,0:T(8,128)} %bitcast.11, f32[2304,256]{1,0:T(8,128)} %bitcast.12), custom_call_target="tpu_custom_call" | custom-call | bytes 23592960 | tf_op jit(solution)/shard_map/pallas_call | solution.py:596
  142.7 0.0 copy-start
  142.7 3.2 %copy.8 = f32[3,3,256,256]{2,3,1,0:T(8,128)} copy(f32[3,3,256,256]{3,2,1,0:T(8,128)} %bitcast.14) | data formatting | bytes 4718592 | tf_op jit(solution)/shard_map/reshape | solution.py:634
  145.9 0.0 copy-done
  145.9 0.0 copy-start.1
  145.9 1.9 %copy.9 = f32[3,3,256,256]{2,3,1,0:T(8,128)} copy(f32[3,3,256,256]{3,2,1,0:T(8,128)S(1)} %bitcast.13) | data formatting | bytes 4718592 | tf_op jit(solution)/shard_map/reshape | solution.py:635
  147.9 0.0 copy-done.1
  147.9 1.0 copy.11
Async XLA Ops:
  142.7 3.2 %copy-start = (f32[2304,256]{1,0:T(8,128)S(1)}, f32[2304,256]{1,0:T(8,128)}, u32[]{:S(2)}) copy-start(f32[2304,256]{1,0:T(8,128)} %get-tuple-element.12) | copy-start | bytes 7077892
  145.9 1.9 %copy-start.1 = (bf16[2048,256]{1,0:T(8,128)(2,1)S(1)}, bf16[2048,256]{1,0:T(8,128)(2,1)}, u32[]{:S(2)}) copy-start(bf16[2048,256]{1,0:T(8,128)(2,1)} %get-tuple-element.8) | copy-start | bytes 3145732

commit v4 on v3

--- a/solution.py
+++ b/solution.py
@@ -169,25 +169,30 @@
     )
 
 
-def add_grad(shifts, c, cols, d_ref, flipped, sums):
+def add_grad(shifts, c, cols, d_ref, flipped, sums, after=None):
     rows, chans = shifts.shape[2:]
     span = cols * rows
     for k in range(span // 256):
         flipped[:, k * 256 : (k + 1) * 256] = d_ref[k * 256 : (k + 1) * 256].T
-    for q in range(3):
-        for p in range(3):
+    outs = flipped.shape[0]
+    for p in range(3):
+        for q in range(3):
             piece = shifts[q, pl.ds(c + p, cols)].reshape(span, chans)
-            sums[p, q] += jnp.dot(flipped[...], piece, preferred_element_type=F32)
+            at = (3 * p + q) * outs
+            sums[at : at + outs] += jnp.dot(flipped[...], piece, preferred_element_type=F32)
+        if after is not None:
+            next(after)
 
 
 def main_kernel(
+    pieces, nx,
     x_hbm, w1_ref, w2_ref, w2b_ref, cot_ref,
     feat_ref, g1_ref, g2_ref,
     xs, cs, hs, xstage, xhalo, cstage, chalo, hstage, hhalo,
     give, got, part, mid, landed, own, back, dall, flipped,
     load_sem, row_send, row_recv, col_send, col_recv,
     give_send, give_recv, mid_send, mid_recv,
-    far_send, far_recv, near_send, near_recv, pass_send, pass_recv,
+    far_send, far_recv, near_send, near_recv, pass_send, pass_recv, *sum_refs,
 ):
     freq, nf = lax.axis_index("freq"), lax.axis_size("freq")
     sky, ns = lax.axis_index("sky"), lax.axis_size("sky")
@@ -209,7 +214,10 @@
     greet(
         [("freq", lax.rem(freq + k, nf)) for k in range(1, nf)]
         + [("sky", lax.rem(sky + 1, ns)), ("sky", lax.rem(sky + ns - 1, ns))]
+        + [("sky", sky // nx * nx + lax.rem(sky % nx + k, nx)) for k in range(1, nx)]
+        + [("sky", lax.rem(sky + k * nx, ns)) for k in range(1, ns // nx)]
     )
+    sums = sum_steps(pieces, nx, g1_ref, g2_ref, sum_refs)
     send_columns(cs, strip, col_send.at[0], col_recv.at[0])
     load.wait()
     take_edges(xs, xstage)
@@ -320,15 +328,21 @@
     near.wait_recv()
     add_grad(xs, partner * strip, strip, dall.at[partner], flipped, g1_ref)
     add_grad(hs, 0, strip, cot_ref.reshape(strip * rows, -1), flipped, g2_ref)
+    next(sums)
     for dy in range(1, ny):
         far_copy(dy).wait_recv()
         pass_copy(dy).start()
         owner = lax.rem(y + ny - dy, ny) * 2
         add_grad(xs, (owner + core) * strip, strip, dall.at[owner + core], flipped, g1_ref)
+    next(sums)
     for dy in range(1, ny):
         pass_copy(dy).wait_recv()
         owner = lax.rem(y + ny - dy, ny) * 2
-        add_grad(xs, (owner + 1 - core) * strip, strip, dall.at[owner + 1 - core], flipped, g1_ref)
+        other = owner + 1 - core
+        after = sums if dy == ny - 1 else None
+        add_grad(xs, other * strip, strip, dall.at[other], flipped, g1_ref, after)
+    for _ in sums:
+        pass
 
     def drain(t, carry):
         give_copy(t).wait_send()
@@ -358,12 +372,30 @@
     wide, thin = count + BLOCK, strip + BLOCK
     vmem = pl.BlockSpec(memory_space=pltpu.VMEM)
     dma = pltpu.SemaphoreType.DMA
+    ns = lax.axis_size("sky")
+    nz = 4 if ns % 4 == 0 else 1
+    nx = ns // nz
+    half, chunk = 9 * outs // 2, 9 * outs // nf
+    last = -(-chunk // (16 * ns)) * 16 * ns
+    cut = 3 * hid
+    pieces = [(i * cut, cut) for i in range(3)] + [(0, last)]
+    buffers = []
+    for i, (_, part) in enumerate(pieces):
+        cols = chans if i < 3 else hid
+        buffers += [
+            pltpu.VMEM((part, cols), BF16),
+            pltpu.VMEM((nx - 1, part // nx, cols), BF16),
+            pltpu.VMEM((part // nx, cols), F32),
+            pltpu.VMEM((part // nx, cols), BF16),
+            pltpu.VMEM((nz - 1, part // ns, cols), BF16),
+            pltpu.VMEM((part, cols), BF16),
+        ]
     return pl.pallas_call(
-        main_kernel,
+        functools.partial(main_kernel, pieces, nx),
         out_shape=(
             jax.ShapeDtypeStruct((strip * rows, outs), BF16),
-            jax.ShapeDtypeStruct((3, 3, hid, chans), F32),
-            jax.ShapeDtypeStruct((3, 3, outs, hid), F32),
+            jax.ShapeDtypeStruct((9 * hid, chans), F32),
+            jax.ShapeDtypeStruct((9 * outs, hid), F32),
         ),
         in_specs=[pl.BlockSpec(memory_space=pl.ANY)] + [vmem] * 4,
         out_specs=(vmem,) * 3,
@@ -390,7 +422,19 @@
             dma((3, 2)), dma((3, 2)), dma((2, 2)), dma((2, 2)),
             dma((steps,)), dma((steps,)), dma((away,)), dma((away,)),
             dma((ny - 1,)), dma((ny - 1,)), dma, dma, dma((ny - 1,)), dma((ny - 1,)),
-        ],
+            pltpu.VMEM((half, hid), BF16),
+            pltpu.VMEM((half, hid), BF16),
+            pltpu.VMEM((half, hid), F32),
+            pltpu.VMEM((half, hid), BF16),
+            pltpu.VMEM((ny - 1, chunk, hid), BF16),
+            pltpu.VMEM((last, hid), F32),
+            pltpu.VMEM((9 * outs, hid), BF16),
+            dma((2, 2)),
+            dma((4, ny - 1)),
+            dma((4, 4, nx - 1)),
+            dma((4, 4, nz - 1)),
+        ]
+        + buffers,
         compiler_params=pltpu.CompilerParams(
             collective_id=1, has_side_effects=True, vmem_limit_bytes=VMEM_LIMIT
         ),
@@ -400,8 +444,9 @@
     )(x, w1, w2, w2b, cot)
 
 
-def sum_kernel(pieces, nx, g1_ref, g2_ref, o1_ref, o2_ref, *refs):
+def sum_steps(pieces, nx, g1_ref, g2_ref, refs):
     refs = list(refs)
+    o1_ref, o2_ref = g1_ref, g2_ref
     freq, nf = lax.axis_index("freq"), lax.axis_size("freq")
     sky, ns = lax.axis_index("sky"), lax.axis_size("sky")
     ny, nz = nf // 2, ns // nx
@@ -436,16 +481,11 @@
     def y_peer(k):
         return lax.rem(y + k, ny)
 
-    greet(
-        [("freq", partner)]
-        + [("freq", y_peer(k) * 2 + core) for k in range(1, ny)]
-        + [("sky", x_peer(k)) for k in range(1, nx)]
-        + [("sky", z_peer(k)) for k in range(1, nz)]
-    )
     done = []
     side[...] = g2_ref[rows_of(1 - core, half)].astype(BF16)
     core_out = remote(side, side_in, core_sems.at[0, 0], core_sems.at[0, 1], "freq", partner)
     done += start([core_out])
+    yield
 
     def x_scatter(i):
         src, land_x = sets[i][0], sets[i][1]
@@ -483,11 +523,6 @@
 
     count = len(pieces)
     flights = {}
-    for i in range(count - 1):
-        first, size = pieces[i]
-        sets[i][0][...] = g1_ref[first : first + size].astype(BF16)
-        flights[i] = x_scatter(i)
-
     core_out.wait_recv()
     mine2[...] = g2_ref[rows_of(core, half)] + side_in[...].astype(F32)
     side_y[...] = mine2[...].astype(BF16)
@@ -497,6 +532,12 @@
                "freq", y_peer(k) * 2 + core)
         for k in range(1, ny)
     ])
+    yield
+    for i in range(count - 1):
+        first, size = pieces[i]
+        sets[i][0][...] = g1_ref[first : first + size].astype(BF16)
+        flights[i] = x_scatter(i)
+        yield
 
     def x_sum(i, own):
         size = pieces[i][1] // nx
@@ -514,7 +555,6 @@
         size = rows // nx
         x_sum(i, g1_ref[pl.ds(pl.multiple_of(first + x * size, 16), size)])
 
-    x_sum_first(0)
     land(y_out)
     total = mine2[rows_of(y, chunk)]
     for k in range(ny - 1):
@@ -525,11 +565,11 @@
         joined[chunk:] = jnp.zeros((joined.shape[0] - chunk, joined.shape[1]), F32)
     sets[last][0][...] = joined[...].astype(BF16)
     flights[last] = x_scatter(last)
-    for i in range(1, count - 1):
+    for i in range(count - 1):
         x_sum_first(i)
     x_sum(last, joined[rows_of(x, pieces[last][1] // nx)])
 
-    order = [0, last] + list(range(1, count - 1))
+    order = [0, 1, last] + list(range(2, count - 1))
     for i in order:
         size = pieces[i][1] // ns
         land(flights[i])
@@ -569,70 +609,14 @@
         copy.wait_send()
 
 
-def sum_call(g1, g2):
-    nf, ns = lax.axis_size("freq"), lax.axis_size("sky")
-    ny = nf // 2
-    nz = 4 if ns % 4 == 0 else 1
-    nx = ns // nz
-    rows1, cols1 = g1.shape
-    rows2, cols2 = g2.shape
-    half, chunk = rows2 // 2, rows2 // nf
-    last = -(-chunk // (16 * ns)) * 16 * ns
-    cut = rows1 // 3
-    pieces = [(i * cut, cut) for i in range(3)] + [(0, last)]
-    vmem = pl.BlockSpec(memory_space=pltpu.VMEM)
-    dma = pltpu.SemaphoreType.DMA
-    buffers = []
-    for i, (_, size) in enumerate(pieces):
-        cols = cols1 if i < 3 else cols2
-        buffers += [
-            pltpu.VMEM((size, cols), BF16),
-            pltpu.VMEM((nx - 1, size // nx, cols), BF16),
-            pltpu.VMEM((size // nx, cols), F32),
-            pltpu.VMEM((size // nx, cols), BF16),
-            pltpu.VMEM((nz - 1, size // ns, cols), BF16),
-            pltpu.VMEM((size, cols), BF16),
-        ]
-    return pl.pallas_call(
-        functools.partial(sum_kernel, pieces, nx),
-        out_shape=(
-            jax.ShapeDtypeStruct((rows1, cols1), F32),
-            jax.ShapeDtypeStruct((rows2, cols2), F32),
-        ),
-        in_specs=[vmem] * 2,
-        out_specs=(vmem,) * 2,
-        scratch_shapes=[
-            pltpu.VMEM((half, cols2), BF16),
-            pltpu.VMEM((half, cols2), BF16),
-            pltpu.VMEM((half, cols2), F32),
-            pltpu.VMEM((half, cols2), BF16),
-            pltpu.VMEM((ny - 1, chunk, cols2), BF16),
-            pltpu.VMEM((last, cols2), F32),
-            pltpu.VMEM((rows2, cols2), BF16),
-            dma((2, 2)),
-            dma((4, ny - 1)),
-            dma((4, 4, nx - 1)),
-            dma((4, 4, nz - 1)),
-        ]
-        + buffers,
-        compiler_params=pltpu.CompilerParams(
-            collective_id=0, has_side_effects=True, vmem_limit_bytes=VMEM_LIMIT
-        ),
-        cost_estimate=pl.CostEstimate(flops=0, bytes_accessed=40 * g1.size, transcendentals=0),
-    )(g1, g2)
-
-
 def body(sky_cube, weight_first, weight_second, cotangent):
     strip, rows, _ = cotangent.shape
     weight_back = jnp.transpose(weight_second[::-1, ::-1], (0, 1, 3, 2))
     features, first, second = main_call(
         sky_cube, weight_first, weight_second, weight_back, cotangent
     )
-    sum_first, sum_second = sum_call(
-        first.reshape(-1, first.shape[3]), second.reshape(-1, second.shape[3])
-    )
-    grad_first = jnp.transpose(sum_first.reshape(first.shape), (0, 1, 3, 2))
-    grad_second = jnp.transpose(sum_second.reshape(second.shape), (0, 1, 3, 2))
+    grad_first = jnp.transpose(first.reshape(3, 3, -1, first.shape[1]), (0, 1, 3, 2))
+    grad_second = jnp.transpose(second.reshape(3, 3, -1, second.shape[1]), (0, 1, 3, 2))
     return (features.reshape(strip, rows, -1), grad_first, grad_second)
 
 

time: 149 us -> 144 us (0.966)
  Pallas kernels: 139 us -> 135 us
    pallas_call x2 -> x1, Pallas kernels: 139 us -> 135 us  [main_call(): pl.pallas_call(functools.partial(main_kernel, pieces, nx), out_shape=(jax...]
where the time goes in v4:
time: 144 us
  Pallas kernels  135 us (94%)
  local copies, waits for them, and re-layouts  8.79 us (6%)
    pallas_call x1, Pallas kernels, main_call(): pl.pallas_call(functools.partial(main_kernel, pieces, nx), out_shape=(jax...  135 us
    reshape x1, local copies, waits for them, and re-layouts, body(): first.reshape(3, 3, -1, first.shape[1])  3.2 us

profile of v4, /device:TPU:1, one launch (start us, length us, event | category | flops | bytes accessed | tf_op | source)
XLA Modules:
  0.0 144.1 jit_solution(5162808815065885518)
XLA Ops:
  0.6 1.6 %copy.7 = bf16[3,3,256,256]{2,3,1,0:T(8,128)(2,1)S(1)} copy(bf16[3,3,256,256]{3,2,1,0:T(8,128)(2,1)} %w2_ref.1) | data formatting | bytes 2359296 | tf_op args[2]
  2.2 1.1 reverse_bitcast_fusion.w2b_ref
  3.3 134.6 %shard_map.67 = (bf16[2048,256]{1,0:T(8,128)(2,1)}, f32[2304,256]{1,0:T(8,128)}, f32[2304,256]{1,0:T(8,128)}) custom-call(bf16[256,32,256]{2,1,0:T(8,128)(2,1)} %x_hbm.1, bf16[3,3,256,256]{3,2,1,0:T(8,128)(2,1)} %w1_ref.1, bf16[3,3,256,256]{3,2,1,0:T(8,128)(2,1)} %w2_ref.1, bf16[3,3,256,256]{3,2,1,0:T(8,128)(2,1)} %reverse_bitcast_fusion.w2b_ref, ...), custom_call_target="tpu_custom_call" | custom-call | flops 19327352832 | bytes 8388608 | tf_op jit(solution)/shard_map/pallas_call | solution.py:393
  137.9 0.0 copy-start
  138.0 3.2 %copy.8 = f32[3,3,256,256]{2,3,1,0:T(8,128)} copy(f32[3,3,256,256]{3,2,1,0:T(8,128)} %bitcast.10) | data formatting | bytes 4718592 | tf_op jit(solution)/shard_map/reshape | solution.py:618
  141.2 0.0 copy-done
  141.2 0.0 copy-start.1
  141.2 1.9 %copy.9 = f32[3,3,256,256]{2,3,1,0:T(8,128)} copy(f32[3,3,256,256]{3,2,1,0:T(8,128)S(1)} %bitcast.9) | data formatting | bytes 4718592 | tf_op jit(solution)/shard_map/reshape | solution.py:619
  143.1 0.0 copy-done.1
  143.1 1.0 copy.11
Async XLA Ops:
  137.9 3.2 %copy-start = (f32[2304,256]{1,0:T(8,128)S(1)}, f32[2304,256]{1,0:T(8,128)}, u32[]{:S(2)}) copy-start(f32[2304,256]{1,0:T(8,128)} %get-tuple-element.8) | copy-start | bytes 7077892
  141.2 1.9 %copy-start.1 = (bf16[2048,256]{1,0:T(8,128)(2,1)S(1)}, bf16[2048,256]{1,0:T(8,128)(2,1)}, u32[]{:S(2)}) copy-start(bf16[2048,256]{1,0:T(8,128)(2,1)} %get-tuple-element.6) | copy-start | bytes 3145732
